TPU v7x, 256 devices: a whole 4x4x8 slice. The times are simulated.
256 devices in a mesh: dp: 16 (over z_lo, x, core), tensor: 16 (over y, z_hi).
Axes of the slice: x: 4, y: 4, z: 8 (z_hi: 4, z_lo: 2; z = z_hi * 2 + z_lo), core: 2. Of those that a mesh axis runs over, the one named last changes fastest.
Arguments:
- hidden: bfloat16 [6144, 8192], P('dp', 'tensor'), may hold values from -6 to 6
- base_weight: bfloat16 [8192, 8192], P(None, 'tensor'), may hold values from -0.0625 to 0.0625
- generators: float32 [8, 64, 8192], P(None, None, 'tensor'), may hold values from -0.24 to 0.24
- cotangent: bfloat16 [6144, 8192], P('dp', 'tensor'), may hold values from -6 to 6
Outputs:
- query: bfloat16 [6144, 8192], P('dp', 'tensor')
- input_grad: bfloat16 [6144, 8192], P('dp', 'tensor')
- factor_grad: float32 [8, 64, 8192], P(None, None, 'tensor')
All inputs are finite; a program needn't handle non-finite values.
Results may differ from a plain program's by a relative error of at most 0.0065.
Values may be sent and summed in bfloat16 or wider, within the bound.
A program may use at most 128 MiB of HBM per device.

v0:
```python
import math

import jax
import jax.numpy as jnp
from jax import lax
from jax.sharding import PartitionSpec as P


def from_partner(value, axis, distance):
    mask = 2**distance
    pairs = [(source, source ^ mask) for source in range(lax.axis_size(axis))]
    return lax.ppermute(value, axis, pairs)


def pair_flip(values, stride):
    count, groups, half_block = values.shape
    shaped = values.reshape(count, groups // (2 * stride), 2, stride, half_block)
    return shaped[:, :, ::-1].reshape(count, groups, half_block)


def apply_mix(low_half, high_half, factor):
    half_block = factor.shape[0] // 2
    mixed = jnp.einsum(
        "nci,icr->ncr", low_half, factor[:half_block], precision=lax.Precision.HIGHEST
    )
    return mixed + jnp.einsum(
        "nci,icr->ncr", high_half, factor[half_block:], precision=lax.Precision.HIGHEST
    )


def mix_backward(grad_out, low_half, high_half, factor):
    half_block = factor.shape[0] // 2
    d_low = jnp.einsum(
        "ncr,icr->nci", grad_out, factor[:half_block], precision=lax.Precision.HIGHEST
    )
    d_high = jnp.einsum(
        "ncr,icr->nci", grad_out, factor[half_block:], precision=lax.Precision.HIGHEST
    )
    g_low = jnp.einsum("nci,ncr->icr", low_half, grad_out, precision=lax.Precision.HIGHEST)
    g_high = jnp.einsum("nci,ncr->icr", high_half, grad_out, precision=lax.Precision.HIGHEST)
    return (d_low, d_high, jnp.concatenate([g_low, g_high], axis=0))


def group_mask(groups, stride):
    return (jnp.arange(groups) // stride % 2 == 1)[None, :, None]


def local_forward(values, factor, stride):
    partner = pair_flip(values, stride)
    upper_mask = group_mask(values.shape[1], stride)
    low_half = jnp.where(upper_mask, partner, values)
    high_half = jnp.where(upper_mask, values, partner)
    return (values + apply_mix(low_half, high_half, factor), low_half, high_half)


def local_backward(grad_out, low_half, high_half, factor, stride):
    d_low, d_high, g_factor = mix_backward(grad_out, low_half, high_half, factor)
    upper_mask = group_mask(grad_out.shape[1], stride)
    own_part = jnp.where(upper_mask, d_high, d_low)
    other_part = jnp.where(upper_mask, d_low, d_high)
    return (grad_out + own_part + pair_flip(other_part, stride), g_factor)


def on_device(hidden, base_weight, generators, cotangent):
    tok_rows = hidden.shape[0]
    col_width = base_weight.shape[1]
    num_factors = generators.shape[0]
    half_block = generators.shape[1] // 2
    local_groups = col_width // half_block
    my_index = lax.axis_index("tensor")
    local_count = local_groups.bit_length() - 1
    cross_count = num_factors - local_count
    token_total = tok_rows * lax.axis_size("dp")
    weight_rows = base_weight
    base = jnp.dot(
        lax.all_gather(hidden, "tensor", axis=1, tiled=True),
        weight_rows,
        preferred_element_type=jnp.float32,
    )
    params = generators.reshape(num_factors, 2 * half_block, local_groups, half_block)
    values = base.reshape(tok_rows, local_groups, half_block)
    saved_low = []
    saved_high = []
    for factor_idx in range(local_count):
        values, low_half, high_half = local_forward(values, params[factor_idx], 2**factor_idx)
        saved_low.append(low_half)
        saved_high.append(high_half)
    grad_list = [None] * num_factors
    for bit_pos in range(cross_count):
        partner = from_partner(values.astype(jnp.bfloat16), "tensor", bit_pos).astype(values.dtype)
        upper_bit = my_index >> bit_pos & 1 == 1
        low_half = jnp.where(upper_bit, partner, values)
        high_half = jnp.where(upper_bit, values, partner)
        values = values + apply_mix(low_half, high_half, params[local_count + bit_pos])
        saved_low.append(low_half)
        saved_high.append(high_half)
    query = values.reshape(tok_rows, col_width).astype(jnp.bfloat16)
    grad_vals = cotangent.astype(jnp.float32).reshape(tok_rows, local_groups, half_block)
    for bit_pos in reversed(range(cross_count)):
        factor_idx = local_count + bit_pos
        d_low, d_high, g_factor = mix_backward(
            grad_vals, saved_low[factor_idx], saved_high[factor_idx], params[factor_idx]
        )
        upper_bit = my_index >> bit_pos & 1 == 1
        own_part = jnp.where(upper_bit, d_high, d_low)
        other_part = jnp.where(upper_bit, d_low, d_high)
        returned = from_partner(other_part, "tensor", bit_pos)
        grad_vals = grad_vals + own_part + returned
        grad_list[factor_idx] = g_factor
    for factor_idx in reversed(range(local_count)):
        grad_vals, g_factor = local_backward(
            grad_vals,
            saved_low[factor_idx],
            saved_high[factor_idx],
            params[factor_idx],
            2**factor_idx,
        )
        grad_list[factor_idx] = g_factor
    stacked = jnp.stack(grad_list, axis=0).reshape(num_factors, 2 * half_block, col_width)
    factor_grad = lax.psum(stacked, "dp") * (1.0 / math.sqrt(token_total))
    base_grad_b = grad_vals.reshape(tok_rows, col_width).astype(jnp.bfloat16)
    weight_rows = base_weight
    summed = lax.psum_scatter(
        lax.dot_general(
            weight_rows, base_grad_b, (((1,), (1,)), ((), ())), preferred_element_type=jnp.float32
        ),
        "tensor",
        scatter_dimension=0,
        tiled=True,
    )
    input_grad = summed.T.astype(jnp.bfloat16)
    return (query, input_grad, factor_grad)


def solution(mesh):
    placed = (P("dp", "tensor"), P(None, "tensor"), P(None, None, "tensor"), P("dp", "tensor"))
    return jax.shard_map(
        on_device,
        mesh=mesh,
        in_specs=placed,
        out_specs=(P("dp", "tensor"), P("dp", "tensor"), P(None, None, "tensor")),
        check_vma=False,
    )
```

profile of v0, /device:TPU:1, one launch (start us, length us, event | category | flops | bytes accessed | tf_op | source)
XLA Modules:
  0.0 669.2 jit_solution(10358698520644446539)
XLA Ops:
  13.6 3.7 collective-permute-start.4
  18.3 17.6 %collective-permute-done.4 = f32[384,16,32]{0,2,1:T(8,128)} collective-permute-done((f32[384,16,32]{0,2,1:T(8,128)}, f32[384,16,32]{0,2,1:T(8,128)}, u32[]{:S(2)}, u32[]{:S(2)}) %collective-permute-start.4) | collective-permute-done | bytes 786464 | tf_op jit(solution)/shard_map/ppermute | solution.py:12
  45.6 14.6 %collective-permute-done.5 = f32[384,16,32]{0,2,1:T(8,128)} collective-permute-done((f32[384,16,32]{0,2,1:T(8,128)S(1)}, f32[384,16,32]{0,2,1:T(8,128)}, u32[]{:S(2)}, u32[]{:S(2)}) %collective-permute-start.5) | collective-permute-done | bytes 786464 | tf_op jit(solution)/shard_map/ppermute | solution.py:12
  66.1 5.1 collective-permute-start.6
  74.6 42.8 %collective-permute-done.6 = f32[384,16,32]{0,2,1:T(8,128)} collective-permute-done((f32[384,16,32]{0,2,1:T(8,128)S(1)}, f32[384,16,32]{0,2,1:T(8,128)}, u32[]{:S(2)}, u32[]{:S(2)}) %collective-permute-start.6) | collective-permute-done | bytes 786464 | tf_op jit(solution)/shard_map/ppermute | solution.py:12
  124.5 17.6 %collective-permute-start.7 = (f32[384,16,32]{0,2,1:T(8,128)}, f32[384,16,32]{0,2,1:T(8,128)}, u32[]{:S(2)}, u32[]{:S(2)}) collective-permute-start(f32[384,16,32]{0,2,1:T(8,128)} %select_bitcast_fusion), channel_id=1, source_target_pairs={{0,1},{1,0},{2,3},{3,2},{4,5},{5,4},{6,7},{7,6},{8,9},{9,8},{10,11... | collective-permute-start | bytes 2359304 | tf_op jit(solution)/shard_map/ppermute | solution.py:12
  155.6 30.2 %collective-permute-done.7 = f32[384,16,32]{0,2,1:T(8,128)} collective-permute-done((f32[384,16,32]{0,2,1:T(8,128)}, f32[384,16,32]{0,2,1:T(8,128)}, u32[]{:S(2)}, u32[]{:S(2)}) %collective-permute-start.7) | collective-permute-done | bytes 786464 | tf_op jit(solution)/shard_map/ppermute | solution.py:12
  190.1 2.9 broadcast_select_fusion.3
  199.0 3.1 broadcast_select_fusion.2
  208.3 3.1 broadcast_select_fusion.1
  217.6 3.1 broadcast_select_fusion
  222.9 11.0 %fusion.54 = f32[384,512]{0,1:T(8,128)} fusion(bf16[384,8192]{1,0:T(8,128)(2,1)} %all-gather.2.cloned.1.call-done, bf16[8192,512]{1,0:T(8,128)(2,1)} %param.5), kind=kOutput, calls=%fused_computation.152 | convolution fusion | flops 3221225472 | bytes 15466496 | tf_op jit(solution)/shard_map/dot_general | solution.py:75
  236.0 3.4 bitcast_select_fusion.6
  239.4 2.9 convolution_bitcast_fusion.16
  250.4 2.9 convolution_bitcast_fusion.14
  255.0 2.9 convolution_bitcast_fusion.13
  263.4 2.9 convolution_bitcast_fusion.12
  268.1 3.0 convolution_bitcast_fusion.11
  274.9 2.5 bitcast_select_fusion
  279.1 2.7 fusion.58
  287.5 3.3 fusion.50
  310.0 3.3 fusion.51
  315.5 2.3 convolution_bitcast_fusion.8
  318.7 9.3 %collective-permute-done.1 = bf16[384,16,32]{0,2,1:T(8,128)(2,1)} collective-permute-done((bf16[384,16,32]{0,2,1:T(8,128)(2,1)}, bf16[384,16,32]{0,2,1:T(8,128)(2,1)}, u32[]{:S(2)}, u32[]{:S(2)}) %collective-permute-start.1) | collective-permute-done | bytes 393248 | tf_op jit(solution)/shard_map/ppermute | solution.py:12
  329.9 2.7 fusion.52
  341.5 2.7 fusion.53
  344.2 2.5 collective-permute-start.3
  351.8 3.4 collective-permute-done.3
  357.4 11.6 %convolution_bitcast_fusion = f32[8192,384]{0,1:T(8,128)} fusion(bf16[384,512]{0,1:T(8,128)(2,1)} %bitcast.308, bf16[8192,512]{1,0:T(8,128)(2,1)} %param.5), kind=kOutput, calls=%fused_computation | convolution fusion | flops 3221225472 | bytes 21364736 | tf_op jit(solution)/shard_map/dot_general | solution.py:124
  372.7 121.4 %all-reduce.2.cloned.1.call-done = f32[8,64,512]{2,1,0:T(8,128)} async-done(((f32[8,64,512]{2,1,0:T(8,128)}), f32[8,64,512]{2,1,0:T(8,128)}) %all-reduce.2.cloned.1.call-update) | async-done | bytes 1048592 | tf_op jit(solution)/shard_map/psum | solution.py:120
  494.1 2.3 broadcast_multiply_fusion
  496.4 163.9 %reduce-scatter.2.cloned.1.call-done = f32[512,384]{0,1:T(8,128)} async-done(((f32[8192,384]{0,1:T(8,128)}), f32[512,384]{0,1:T(8,128)}) %reduce-scatter.2.cloned.1.call-update) | async-done | bytes 786448 | tf_op jit(solution)/shard_map/reduce_scatter | solution.py:123
  (163 shorter events, 147.7 us)
Async XLA Ops:
  7.2 215.7 %all-gather.2.cloned.1.call-start = ((), (), s32[]{:S(2)}) async-start(), calls=%async_computation.1 | async-start | bytes 6684672 | tf_op jit(solution)/shard_map/all_gather | solution.py:76
  7.9 486.2 %all-reduce.2.cloned.1.call-start = ((), (), s32[]{:S(2)}) async-start(), calls=%async_computation.3 | async-start | bytes 2097152 | tf_op jit(solution)/shard_map/psum | solution.py:120
  11.4 6.9 %copy-start.22 = (f32[1,32,512]{1,2,0:T(8,128)}, f32[1,32,512]{1,2,0:T(8,128)S(1)}, u32[]{:S(2)}) copy-start(f32[1,32,512]{1,2,0:T(8,128)S(1)} %copy.69) | copy-start | bytes 196612
  11.5 6.8 %copy-start.17 = (f32[1,32,512]{1,2,0:T(8,128)}, f32[1,32,512]{1,2,0:T(8,128)S(1)}, u32[]{:S(2)}) copy-start(f32[1,32,512]{1,2,0:T(8,128)S(1)} %copy.70) | copy-start | bytes 196612
  13.6 22.4 %collective-permute-start.4 = (f32[384,16,32]{0,2,1:T(8,128)}, f32[384,16,32]{0,2,1:T(8,128)}, u32[]{:S(2)}, u32[]{:S(2)}) collective-permute-start(f32[384,16,32]{0,2,1:T(8,128)} %select_bitcast_fusion.3), channel_id=1, source_target_pairs={{0,8},{1,9},{2,10},{3,11},{4,12},{5,13},{6,14},{7,15},{8,0},{9,1},... | collective-permute-start | bytes 2359304 | tf_op jit(solution)/shard_map/ppermute | solution.py:12
  18.3 19.9 %copy-start.15 = (f32[1,32,512]{1,2,0:T(8,128)}, f32[1,32,512]{1,2,0:T(8,128)S(1)}, u32[]{:S(2)}) copy-start(f32[1,32,512]{1,2,0:T(8,128)S(1)} %copy.67) | copy-start | bytes 196612
  40.1 20.1 %collective-permute-start.5 = (f32[384,16,32]{0,2,1:T(8,128)S(1)}, f32[384,16,32]{0,2,1:T(8,128)}, u32[]{:S(2)}, u32[]{:S(2)}) collective-permute-start(f32[384,16,32]{0,2,1:T(8,128)S(1)} %select_bitcast_fusion.2), channel_id=1, source_target_pairs={{0,4},{1,5},{2,6},{3,7},{4,0},{5,1},{6,2},{7,3},{8,12},{9,13},{10,... | collective-permute-start | bytes 2359304 | tf_op jit(solution)/shard_map/ppermute | solution.py:12
  66.1 51.3 %collective-permute-start.6 = (f32[384,16,32]{0,2,1:T(8,128)S(1)}, f32[384,16,32]{0,2,1:T(8,128)}, u32[]{:S(2)}, u32[]{:S(2)}) collective-permute-start(f32[384,16,32]{0,2,1:T(8,128)S(1)} %select_bitcast_fusion.1), channel_id=1, source_target_pairs={{0,2},{1,3},{2,0},{3,1},{4,6},{5,7},{6,4},{7,5},{8,10},{9,11},{10,... | collective-permute-start | bytes 2359304 | tf_op jit(solution)/shard_map/ppermute | solution.py:12
  120.6 35.0 %copy-start.7 = (f32[16,384,32]{1,2,0:T(8,128)}, f32[16,384,32]{1,2,0:T(8,128)S(1)}, u32[]{:S(2)}) copy-start(f32[16,384,32]{1,2,0:T(8,128)S(1)} %fusion.66) | copy-start | bytes 2359300
  124.5 61.3 %collective-permute-start.7 = (f32[384,16,32]{0,2,1:T(8,128)}, f32[384,16,32]{0,2,1:T(8,128)}, u32[]{:S(2)}, u32[]{:S(2)}) collective-permute-start(f32[384,16,32]{0,2,1:T(8,128)} %select_bitcast_fusion), channel_id=1, source_target_pairs={{0,1},{1,0},{2,3},{3,2},{4,5},{5,4},{6,7},{7,6},{8,9},{9,8},{10,11... | collective-permute-start | bytes 2359304 | tf_op jit(solution)/shard_map/ppermute | solution.py:12
  189.2 1.0 copy-start.10
  197.0 2.0 copy-start
  199.0 3.2 copy-start.11
  206.3 2.0 copy-start.1
  208.3 3.2 copy-start.12
  215.6 2.0 copy-start.2
  217.6 3.2 copy-start.13
  236.0 6.3 copy-start.16
  236.0 7.1 %copy-start.3 = (f32[384,16,32]{0,2,1:T(8,128)S(1)}, f32[384,16,32]{0,2,1:T(8,128)}, u32[]{:S(2)}) copy-start(f32[384,16,32]{0,2,1:T(8,128)} %copy-done.2) | copy-start | bytes 2359300
  236.0 8.9 %copy-start.14 = (f32[384,512]{0,1:T(8,128)S(1)}, f32[384,512]{0,1:T(8,128)}, u32[]{:S(2)}) copy-start(f32[384,512]{0,1:T(8,128)} %fusion.54) | copy-start | bytes 2359300
  236.0 8.9 %copy-start.21 = (f32[1,32,512]{1,2,0:T(8,128)S(1)}, f32[1,32,512]{1,2,0:T(8,128)}, u32[]{:S(2)}) copy-start(f32[1,32,512]{1,2,0:T(8,128)} %copy.56) | copy-start | bytes 196612
  248.7 9.2 %copy-start.5 = (f32[384,16,32]{0,2,1:T(8,128)S(1)}, f32[384,16,32]{0,2,1:T(8,128)}, u32[]{:S(2)}) copy-start(f32[384,16,32]{0,2,1:T(8,128)} %fusion.15) | copy-start | bytes 2359300
  248.7 9.2 %copy-start.20 = (f32[1,32,512]{1,2,0:T(8,128)S(1)}, f32[1,32,512]{1,2,0:T(8,128)}, u32[]{:S(2)}) copy-start(f32[1,32,512]{1,2,0:T(8,128)} %copy.58) | copy-start | bytes 196612
  261.8 9.3 %copy-start.6 = (f32[384,16,32]{0,2,1:T(8,128)S(1)}, f32[384,16,32]{0,2,1:T(8,128)}, u32[]{:S(2)}) copy-start(f32[384,16,32]{0,2,1:T(8,128)} %fusion.13) | copy-start | bytes 2359300
  261.8 9.3 %copy-start.19 = (f32[1,32,512]{1,2,0:T(8,128)S(1)}, f32[1,32,512]{1,2,0:T(8,128)}, u32[]{:S(2)}) copy-start(f32[1,32,512]{1,2,0:T(8,128)} %copy.60) | copy-start | bytes 196612
  290.8 17.3 %copy-start.4 = (f32[384,16,32]{0,2,1:T(8,128)}, f32[384,16,32]{0,2,1:T(8,128)S(1)}, u32[]{:S(2)}) copy-start(f32[384,16,32]{0,2,1:T(8,128)S(1)} %get-tuple-element.43) | copy-start | bytes 2359300
  290.8 17.3 %collective-permute-start = (bf16[384,16,32]{0,2,1:T(8,128)(2,1)}, bf16[384,16,32]{0,2,1:T(8,128)(2,1)}, u32[]{:S(2)}, u32[]{:S(2)}) collective-permute-start(bf16[384,16,32]{0,2,1:T(8,128)(2,1)} %get-tuple-element.42), channel_id=1, source_target_pairs={{0,1},{1,0},{2,3},{3,2},{4,5},{5,4},{6,7},{7,6},{8,9},{9,8},{10,11... | collective-permute-start | bytes 1179656 | tf_op jit(solution)/shard_map/ppermute | solution.py:12
  313.2 14.8 %collective-permute-start.1 = (bf16[384,16,32]{0,2,1:T(8,128)(2,1)}, bf16[384,16,32]{0,2,1:T(8,128)(2,1)}, u32[]{:S(2)}, u32[]{:S(2)}) collective-permute-start(bf16[384,16,32]{0,2,1:T(8,128)(2,1)} %get-tuple-element.44), channel_id=1, source_target_pairs={{0,2},{1,3},{2,0},{3,1},{4,6},{5,7},{6,4},{7,5},{8,10},{9,11},{10,... | collective-permute-start | bytes 1179656 | tf_op jit(solution)/shard_map/ppermute | solution.py:12
  332.7 6.9 %collective-permute-start.2 = (bf16[384,16,32]{0,2,1:T(8,128)(2,1)}, bf16[384,16,32]{0,2,1:T(8,128)(2,1)}, u32[]{:S(2)}, u32[]{:S(2)}) collective-permute-start(bf16[384,16,32]{0,2,1:T(8,128)(2,1)} %get-tuple-element.46), channel_id=1, source_target_pairs={{0,4},{1,5},{2,6},{3,7},{4,0},{5,1},{6,2},{7,3},{8,12},{9,13},{10,... | collective-permute-start | bytes 1179656 | tf_op jit(solution)/shard_map/ppermute | solution.py:12
  344.2 11.0 %collective-permute-start.3 = (bf16[384,16,32]{0,2,1:T(8,128)(2,1)}, bf16[384,16,32]{0,2,1:T(8,128)(2,1)S(1)}, u32[]{:S(2)}, u32[]{:S(2)}) collective-permute-start(bf16[384,16,32]{0,2,1:T(8,128)(2,1)} %get-tuple-element.48), channel_id=1, source_target_pairs={{0,8},{1,9},{2,10},{3,11},{4,12},{5,13},{6,14},{7,15},{8,0},{9,1},... | collective-permute-start | bytes 1179656 | tf_op jit(solution)/shard_map/ppermute | solution.py:12
  357.4 302.9 %reduce-scatter.2.cloned.1.call-start = ((), (), s32[]{:S(2)}) async-start(), calls=%async_computation.2 | async-start | bytes 13369344 | tf_op jit(solution)/shard_map/reduce_scatter | solution.py:123
  369.0 1.8 copy-start.23
  (3 other events, 2.8 us)
Sparse Core Ops, SparseCore 0:
  10.4 135.6 all-gather.1
  357.5 136.4 all-reduce.1
  498.3 161.9 reduce-scatter.1
where the time goes:
time: 680 us; the launch traced here: 669 us
  waiting for transfers between devices  405 us (60%)
  matrix products  119 us (18%)
  local copies, waits for them, and re-layouts  62.6 us (9%)
  other arithmetic  35.6 us (5%)
  starting transfers between devices  32.4 us (5%)
  between operations  14.8 us (2%)
    reduce_scatter x1, waiting for transfers between devices, on_device(): lax.psum_scatter(lax.dot_general(weight_rows, base_grad_b, (((1,), (1,)),...  164 us
    psum x1, waiting for transfers between devices, on_device(): factor_grad = lax.psum(stacked, 'dp') * (1.0 / math.sqrt(token_total))  121 us
    ppermute x8, waiting for transfers between devices, from_partner(): return lax.ppermute(value, axis, pairs)  119 us
    ppermute x8, starting transfers between devices, from_partner(): return lax.ppermute(value, axis, pairs)  32.2 us
    dot_general x8, matrix products, mix_backward(): jnp.einsum('nci,ncr->icr', low_half, grad_out, precision=lax.Precision.HI...  17.3 us
    dot_general x8, matrix products, mix_backward(): jnp.einsum('ncr,icr->nci', grad_out, factor[:half_block], precision=lax.P...  17.2 us
    rev x8, local copies, waits for them, and re-layouts, pair_flip(): return shaped[:, :, ::-1].reshape(count, groups, half_block)  16.9 us
    dot_general x8, matrix products, apply_mix(): jnp.einsum('nci,icr->ncr', low_half, factor[:half_block], precision=lax.P...  16.6 us
  transfers between devices with their start and end apart: 11, of which 9 were waited for; matrix products, arithmetic and copies ran while one was open for 19% of the time, Pallas kernels for 0%

commit v1 on v0

v1 whole, which is shorter than its diff:
```python
import functools
import math

import jax
import jax.numpy as jnp
from jax import lax
from jax.experimental import pallas as pl
from jax.experimental.pallas import tpu as pltpu
from jax.sharding import PartitionSpec as P

MESH = pl.DeviceIdType.MESH
F32 = jnp.float32
BF16 = jnp.bfloat16
SIDE = 4
LANES = 128
HALF = 32
VMEM_BYTES = 60 * 1024 * 1024


def wrap(value, n):
    return lax.rem(value + n, n)


def dot(a, b):
    return jnp.dot(a, b, preferred_element_type=F32)


def dot_nt(a, b):
    return lax.dot_general(a, b, (((1,), (1,)), ((), ())), preferred_element_type=F32)


def dot_tn(a, b):
    return lax.dot_general(a, b, (((0,), (0,)), ((), ())), preferred_element_type=F32)


def groups_of(shape):
    rows = lax.broadcasted_iota(jnp.int32, shape, 0) >> 5
    cols = lax.broadcasted_iota(jnp.int32, shape, 1) >> 5
    return rows, cols


def spread(block, mask, copies):
    return jnp.where(mask, jnp.concatenate([block] * copies, axis=0), 0.0)


def pair_matrix(gen_a, gen_b):
    both = jnp.concatenate([gen_a, gen_b], axis=1)
    rows, cols = groups_of((LANES, 2 * LANES))
    mask = rows == (cols & 3)
    return jnp.concatenate(
        [spread(both[:HALF], mask, 4), spread(both[HALF:], mask, 4)], axis=0
    ).astype(BF16)


def pair_extract(grad):
    cols = (lax.broadcasted_iota(jnp.int32, (HALF, 2 * LANES), 1) >> 5) & 3
    parts = []
    for h in range(2):
        total = jnp.zeros((HALF, 2 * LANES), F32)
        for g in range(4):
            start = h * LANES + g * HALF
            total = total + jnp.where(cols == g, grad[start : start + HALF], 0.0)
        parts.append(total)
    return jnp.concatenate(parts, axis=0)


def near_matrix(gen, k):
    rows, cols = groups_of((256, 256))
    low = cols & ~(1 << k)
    return (
        spread(gen[:HALF], rows == low, 8) + spread(gen[HALF:], rows == (low | (1 << k)), 8)
    ).astype(BF16)


def near_extract(grad, k):
    cols = lax.broadcasted_iota(jnp.int32, (HALF, 256), 1) >> 5
    low = cols & ~(1 << k)
    parts = []
    for want in (low, low | (1 << k)):
        total = jnp.zeros((HALF, 256), F32)
        for g in range(8):
            total = total + jnp.where(want == g, grad[g * HALF : (g + 1) * HALF], 0.0)
        parts.append(total)
    return jnp.concatenate(parts, axis=0)


def diag_matrix(block):
    rows, cols = groups_of((256, 256))
    return spread(block, rows == cols, 8).astype(BF16)


def diag_extract(grad):
    cols = lax.broadcasted_iota(jnp.int32, (HALF, 256), 1) >> 5
    total = jnp.zeros((HALF, 256), F32)
    for g in range(8):
        total = total + jnp.where(cols == g, grad[g * HALF : (g + 1) * HALF], 0.0)
    return total


class Ids:
    def __init__(self):
        self.next = 0

    def take(self, n=1):
        first = self.next
        self.next += n
        return first


IDS = Ids()
AG_Z = IDS.take(4)
AG_Y = [IDS.take(4) for _ in range(4)]
RS_Y = [IDS.take(4) for _ in range(4)]
RS_Z = IDS.take(4)
GEN_Z = IDS.take(4)
GEN_Y = IDS.take(4)
COT_Y = IDS.take(4)
BWD_T = IDS.take(4)
BWD_Z = IDS.take(4)
FWD_Z = IDS.take(4)
FWD_T = IDS.take(4)
FWD_Y = IDS.take(4)
OUT_Z = IDS.take(4)
OUT_Y = IDS.take(4)
N_SEMS = IDS.next


def main_kernel(
    hid, wt, gen, cot, query, igrad, ggrad,
    w_v, hbuf, base, gz, gy, gyb, gzb, ghome, gsave_y, gsave_z, glocal, slocal,
    szb, ssend, syb, qsend, qb, s5b, s7b, zsend, gsend_t, gsend_z, gb,
    rs_s2, rs_r2, rs_s1, rs_s3, rs_r1, rs_r3, q_s2, q_r2, q_s1, q_s3, q_r1, q_r3,
    gp, gp_z, gp_y, mats_loc, mats_z, mats_y,
    send_sem, recv_sem, w_sem, l_sem,
):
    tokens = hid.shape[0]
    half = tokens // 2
    me = lax.axis_index("tensor")
    y, z = me // SIDE, lax.rem(me, SIDE)
    upper, lower = pl.ds(0, half), pl.ds(half, half)
    pending = []

    def at(dy, dz):
        return wrap(y + dy, SIDE) * SIDE + wrap(z + dz, SIDE)

    def copy(src, dst, index, dev, slot=None):
        return pltpu.make_async_remote_copy(
            src_ref=src,
            dst_ref=dst,
            send_sem=send_sem.at[index],
            recv_sem=recv_sem.at[index if slot is None else slot],
            device_id={"tensor": dev},
            device_id_type=MESH,
        )

    def send(src, dst, index, dev):
        c = copy(src, dst, index, dev)
        c.start()
        pending.append(c)
        return c

    def w_rows(dy, dz):
        block = at(dy, dz)
        return w_v[pl.ds(pl.multiple_of(block * 512, 512), 512), :]

    w_copy = pltpu.make_async_copy(wt, w_v, w_sem)
    w_copy.start()

    barrier = pltpu.get_barrier_semaphore()
    for d in range(1, 16):
        pl.semaphore_signal(
            barrier, inc=1, device_id={"tensor": lax.rem(me + d, 16)}, device_id_type=MESH
        )
    pl.semaphore_wait(barrier, 15)

    cot_in, genz_in, geny_in = [], [], []
    for d in range(1, 4):
        chunk = lax.rem(y + d + z, SIDE)
        cols = pl.ds(pl.multiple_of(chunk * LANES, LANES), LANES)
        cot_in.append(send(cot.at[:, cols], gyb.at[y], COT_Y + d, at(d, 0)))
        geny_in.append(send(gen.at[pl.ds(6, 2), :, cols], gy.at[y], GEN_Y + d, at(d, 0)))
    own_cols_y = pl.ds(pl.multiple_of(lax.rem(y + z, SIDE) * LANES, LANES), LANES)
    own_cols_z = pl.ds(pl.multiple_of(z * LANES, LANES), LANES)
    for d in range(1, 4):
        cols = pl.ds(pl.multiple_of(wrap(z + d, SIDE) * LANES, LANES), LANES)
        genz_in.append(send(gen.at[pl.ds(4, 2), :, cols], gz.at[z], GEN_Z + d, at(0, d)))

    ag_z = [
        send(hid, hbuf.at[0, 1], AG_Z + 0, at(0, 1)),
        send(hid, hbuf.at[0, 3], AG_Z + 1, at(0, 3)),
    ]
    ag_y = {}

    def ag_spread(dz):
        src = hid if dz == 0 else hbuf.at[0, dz]
        ag_y[dz] = [
            send(src, hbuf.at[1, dz], AG_Y[dz] + 0, at(1, 0)),
            send(src, hbuf.at[3, dz], AG_Y[dz] + 1, at(3, 0)),
        ]

    def ag_forward(dz):
        ag_y[dz][0].wait_recv()
        ag_y[dz].append(
            send(hbuf.at[1, dz, upper], hbuf.at[2, dz, upper], AG_Y[dz] + 2, at(1, 0))
        )
        ag_y[dz][1].wait_recv()
        ag_y[dz].append(
            send(hbuf.at[3, dz, lower], hbuf.at[2, dz, lower], AG_Y[dz] + 3, at(3, 0))
        )

    def accumulate(dy, dz):
        base[...] += dot(hbuf[dy, dz], w_rows(-dy, -dz))

    ag_spread(0)

    gyb[y] = cot[:, own_cols_y]
    gy[y] = gen[6:8, :, own_cols_y]
    gz[z] = gen[4:6, :, own_cols_z]

    for k in range(3):
        for s in range(2):
            mats_loc[k, s] = near_matrix(gen[k, :, 256 * s : 256 * s + 256], k)
    for s in range(2):
        for h in range(2):
            mats_loc[3 + h, s] = diag_matrix(
                gen[3, HALF * h : HALF * h + HALF, 256 * s : 256 * s + 256]
            )

    PAIRS = (((0, 1), (2, 3)), ((0, 2), (1, 3)))

    def pair_of(ref, a, b):
        return jnp.concatenate([ref[a], ref[b]], axis=1)

    for c in geny_in:
        c.wait_recv()
    for k in range(2):
        for i, (a, b) in enumerate(PAIRS[k]):
            mats_y[k, i] = pair_matrix(gy[a, k], gy[b, k])

    for c in cot_in:
        c.wait_recv()

    def pairs_backward(values, mats, save, out):
        for k in (1, 0):
            new = [None] * 4
            for i, (a, b) in enumerate(PAIRS[k]):
                v = jnp.concatenate([values[a], values[b]], axis=1)
                v = v + dot_nt(v.astype(BF16), mats[k, i])
                new[a], new[b] = v[:, :LANES], v[:, LANES:]
            values = new
            target = save if k == 1 else out
            for m in range(4):
                target[m] = values[m].astype(BF16)

    def pairs_forward(values, mats, save, out):
        for k in (0, 1):
            new = [None] * 4
            for i, (a, b) in enumerate(PAIRS[k]):
                v = jnp.concatenate([values[a], values[b]], axis=1)
                v = v + dot(v.astype(BF16), mats[k, i])
                new[a], new[b] = v[:, :LANES], v[:, LANES:]
            values = new
            target = save if k == 0 else out
            for m in range(4):
                target[m] = values[m].astype(BF16)

    def cross(src, dst, first, own_slot, dev_of, src_of):
        sent = []
        for d in range(4):
            c = copy(src.at[src_of(d)], dst.at[own_slot], first + d, dev_of(d), first + own_slot)
            if d == 0:
                keep = pltpu.make_async_copy(
                    src.at[src_of(0)], dst.at[own_slot], recv_sem.at[first + own_slot]
                )
                remote, local = dev_of(0) != me, dev_of(0) == me
                pl.when(remote)(lambda c=c: c.start())
                pl.when(local)(lambda keep=keep: keep.start())
            else:
                c.start()
            sent.append(c)

        def arrive():
            for m in range(4):
                pltpu.make_async_copy(src.at[m], dst.at[m], recv_sem.at[first + m]).wait()

        def finish():
            pl.when(dev_of(0) != me)(lambda: sent[0].wait_send())
            for c in sent[1:]:
                c.wait_send()

        return arrive, finish

    pairs_backward([gyb[m].astype(F32) for m in range(4)], mats_y, gsave_y, gsend_t)
    z_of = lax.rem(y + z, SIDE)
    bwd_arrive, bwd_finish = cross(
        gsend_t, gzb, BWD_T, z,
        lambda d: wrap(y + d, SIDE) * SIDE + z_of,
        lambda d: wrap(y + d, SIDE),
    )

    w_copy.wait()
    base[...] = dot(hid[...], w_rows(0, 0))
    ag_forward(0)
    accumulate(1, 0)
    accumulate(3, 0)

    for c in genz_in:
        c.wait_recv()
    for k in range(2):
        for i, (a, b) in enumerate(PAIRS[k]):
            mats_z[k, i] = pair_matrix(gz[a, k], gz[b, k])

    ag_z[0].wait_recv()
    ag_z.append(send(hbuf.at[0, 1, upper], hbuf.at[0, 2, upper], AG_Z + 2, at(0, 1)))
    ag_spread(1)
    ag_z[1].wait_recv()
    ag_z.append(send(hbuf.at[0, 3, lower], hbuf.at[0, 2, lower], AG_Z + 3, at(0, 3)))
    ag_spread(3)
    accumulate(0, 1)
    accumulate(0, 3)

    bwd_arrive()
    pairs_backward([gzb[m].astype(F32) for m in range(4)], mats_z, gsave_z, gsend_z)
    back_in = []
    for d in range(1, 4):
        back_in.append(
            send(gsend_z.at[wrap(z + d, SIDE)], ghome.at[z], BWD_Z + d, at(0, d))
        )
    ghome[z] = gsend_z[z]

    for c in ag_y[0][2:]:
        c.wait_recv()
    accumulate(2, 0)
    ag_z[2].wait_recv()
    ag_z[3].wait_recv()
    ag_spread(2)
    accumulate(0, 2)
    ag_forward(1)
    accumulate(1, 1)
    accumulate(3, 1)

    for c in back_in:
        c.wait_recv()
    ga = jnp.concatenate([ghome[0], ghome[1]], axis=1)
    gbb = jnp.concatenate([ghome[2], ghome[3]], axis=1)
    glocal[3, 0] = ga
    glocal[3, 1] = gbb
    fa = ga.astype(F32) + dot_nt(ga, mats_loc[3, 0]) + dot_nt(gbb, mats_loc[3, 1])
    fb = gbb.astype(F32) + dot_nt(ga, mats_loc[4, 0]) + dot_nt(gbb, mats_loc[4, 1])
    for k in (2, 1, 0):
        glocal[k, 0] = fa.astype(BF16)
        glocal[k, 1] = fb.astype(BF16)
        fa = fa + dot_nt(glocal[k, 0], mats_loc[k, 0])
        fb = fb + dot_nt(glocal[k, 1], mats_loc[k, 1])
    gb[:, :256] = fa.astype(BF16)
    gb[:, 256:] = fb.astype(BF16)

    ag_forward(3)
    accumulate(1, 3)
    accumulate(3, 3)
    ag_forward(2)
    accumulate(1, 2)
    accumulate(3, 2)

    def part(dy, dz):
        return dot_nt(gb[...], w_rows(dy, dz))

    rs = {}
    ORDER = (2, 1, 3, 0)

    def rs_far(dz):
        rs_s2[dz] = part(2, dz).astype(BF16)
        rs[dz] = [
            send(rs_s2.at[dz, upper], rs_r2.at[dz, 0], RS_Y[dz] + 0, at(1, 0)),
            send(rs_s2.at[dz, lower], rs_r2.at[dz, 1], RS_Y[dz] + 1, at(3, 0)),
        ]

    def rs_near(dz):
        p = part(1, dz)
        rs[dz][0].wait_recv()
        rs_s1[dz, upper] = (p[:half] + rs_r2[dz, 0].astype(F32)).astype(BF16)
        rs_s1[dz, lower] = p[half:].astype(BF16)
        rs[dz].append(send(rs_s1.at[dz], rs_r1.at[dz], RS_Y[dz] + 2, at(1, 0)))
        p = part(3, dz)
        rs[dz][1].wait_recv()
        rs_s3[dz, upper] = p[:half].astype(BF16)
        rs_s3[dz, lower] = (p[half:] + rs_r2[dz, 1].astype(F32)).astype(BF16)
        rs[dz].append(send(rs_s3.at[dz], rs_r3.at[dz], RS_Y[dz] + 3, at(3, 0)))

    def rs_sum(dz):
        p = part(0, dz)
        rs[dz][2].wait_recv()
        rs[dz][3].wait_recv()
        return p + rs_r1[dz].astype(F32) + rs_r3[dz].astype(F32)

    for dz in ORDER:
        rs_far(dz)

    for dz in (1, 3, 2):
        for c in ag_y[dz][2:]:
            c.wait_recv()
        accumulate(2, dz)
    fa, fb = base[:, :256], base[:, 256:]
    for k in range(3):
        slocal[k, 0] = fa.astype(BF16)
        slocal[k, 1] = fb.astype(BF16)
        fa = fa + dot(slocal[k, 0], mats_loc[k, 0])
        fb = fb + dot(slocal[k, 1], mats_loc[k, 1])
    ba, bb = fa.astype(BF16), fb.astype(BF16)
    slocal[3, 0] = ba
    slocal[3, 1] = bb
    fa = fa + dot(ba, mats_loc[3, 0]) + dot(bb, mats_loc[4, 0])
    fb = fb + dot(ba, mats_loc[3, 1]) + dot(bb, mats_loc[4, 1])
    for c in range(4):
        side = fa if c < 2 else fb
        ssend[c] = side[:, (c % 2) * LANES : (c % 2) * LANES + LANES].astype(BF16)
    fwd_in = []
    for d in range(1, 4):
        fwd_in.append(send(ssend.at[wrap(z + d, SIDE)], szb.at[z], FWD_Z + d, at(0, d)))
    szb[z] = ssend[z]

    rs_near(2)
    rs_near(1)

    def put_local(k, s, value):
        for j in range(2):
            gp[(k // 2) * 4 + 2 * s + j, (k % 2) * 64 : (k % 2) * 64 + 64] = value[
                :, j * LANES : (j + 1) * LANES
            ]

    for k in range(3):
        for s in range(2):
            put_local(k, s, near_extract(dot_tn(slocal[k, s], glocal[k, s]), k))
    for s in range(2):
        put_local(
            3, s,
            jnp.concatenate(
                [diag_extract(dot_tn(slocal[3, h], glocal[3, s])) for h in range(2)], axis=0
            ),
        )

    for c in fwd_in:
        c.wait_recv()
    pairs_forward([szb[m].astype(F32) for m in range(4)], mats_z, s5b, zsend)
    fwd_arrive, fwd_finish = cross(
        zsend, syb, FWD_T, y,
        lambda d: ((SIDE - d) % SIDE) * SIDE + wrap(z + d, SIDE),
        lambda d: wrap(z + d, SIDE),
    )

    rs_near(3)
    rs_near(0)

    def pair_grads(states, grads, dst):
        for k in range(2):
            for i, (a, b) in enumerate(PAIRS[k]):
                value = pair_extract(dot_tn(pair_of(states[k], a, b), pair_of(grads[k], a, b)))
                dst[a, k * 64 : k * 64 + 64] = value[:, :LANES]
                dst[b, k * 64 : k * 64 + 64] = value[:, LANES:]

    pair_grads((szb, s5b), (gsave_z, gzb), gp_z)
    outz_in = []
    for d in range(1, 4):
        outz_in.append(send(gp_z.at[wrap(z + d, SIDE)], gp.at[8 + z], OUT_Z + d, at(0, d)))
    gp[8 + z] = gp_z[z]

    fwd_arrive()
    pairs_forward([syb[m].astype(F32) for m in range(4)], mats_y, s7b, qsend)
    query_in = []
    for d in range(1, 4):
        query_in.append(send(qsend.at[wrap(y + d, SIDE)], qb.at[z_of], FWD_Y + d, at(d, 0)))
    qb[z_of] = qsend[y]

    pair_grads((syb, s7b), (gsave_y, gyb), gp_y)
    outy_in = []
    for d in range(1, 4):
        outy_in.append(send(gp_y.at[wrap(y + d, SIDE)], gp.at[12 + z_of], OUT_Y + d, at(d, 0)))
    gp[12 + z_of] = gp_y[y]

    q_s2[...] = rs_sum(2).astype(BF16)
    rz = [
        send(q_s2.at[upper], q_r2.at[0], RS_Z + 0, at(0, 1)),
        send(q_s2.at[lower], q_r2.at[1], RS_Z + 1, at(0, 3)),
    ]
    q = rs_sum(1)
    rz[0].wait_recv()
    q_s1[upper] = (q[:half] + q_r2[0].astype(F32)).astype(BF16)
    q_s1[lower] = q[half:].astype(BF16)
    rz.append(send(q_s1, q_r1, RS_Z + 2, at(0, 1)))
    q = rs_sum(3)
    rz[1].wait_recv()
    q_s3[upper] = q[:half].astype(BF16)
    q_s3[lower] = (q[half:] + q_r2[1].astype(F32)).astype(BF16)
    rz.append(send(q_s3, q_r3, RS_Z + 3, at(0, 3)))
    q = rs_sum(0)

    for c in query_in + outz_in + outy_in:
        c.wait_recv()
    for c in range(4):
        query[:, c * LANES : (c + 1) * LANES] = qb[c]
    ggrad[...] = gp[...]
    rz[2].wait_recv()
    rz[3].wait_recv()
    igrad[...] = (q + q_r1[...].astype(F32) + q_r3[...].astype(F32)).astype(BF16)

    for c in pending:
        c.wait_send()
    bwd_finish()
    fwd_finish()


def main_call(hidden, weight, generators, cotangent):
    tokens = hidden.shape[0]
    half = tokens // 2
    vm = lambda *shape, dtype=BF16: pltpu.VMEM(shape, dtype)
    chunks = vm(4, tokens, LANES)
    block = vm(tokens, 512)
    blocks = vm(4, tokens, 512)
    flops = 4 * tokens * 8192 * 512
    return pl.pallas_call(
        main_kernel,
        out_shape=(
            jax.ShapeDtypeStruct((tokens, 512), BF16),
            jax.ShapeDtypeStruct((tokens, 512), BF16),
            jax.ShapeDtypeStruct((16, 128, 128), F32),
        ),
        in_specs=[
            pl.BlockSpec(memory_space=pltpu.VMEM),
            pl.BlockSpec(memory_space=pl.ANY),
            pl.BlockSpec(memory_space=pltpu.VMEM),
            pl.BlockSpec(memory_space=pltpu.VMEM),
        ],
        out_specs=[pl.BlockSpec(memory_space=pltpu.VMEM)] * 3,
        scratch_shapes=[
            vm(8192, 512),
            vm(4, 4, tokens, 512),
            vm(tokens, 512, dtype=F32),
            vm(4, 2, 64, LANES, dtype=F32),
            vm(4, 2, 64, LANES, dtype=F32),
            chunks, chunks, chunks, chunks, chunks,
            vm(4, 2, tokens, 256),
            vm(4, 2, tokens, 256),
            chunks, chunks, chunks, chunks, chunks,
            chunks, chunks, chunks, chunks, chunks,
            block,
            blocks, vm(4, 2, half, 512), blocks, blocks, blocks, blocks,
            block, vm(2, half, 512), block, block, block, block,
            vm(16, 128, 128, dtype=F32),
            vm(4, 128, 128, dtype=F32),
            vm(4, 128, 128, dtype=F32),
            vm(5, 2, 256, 256),
            vm(2, 2, 256, 256),
            vm(2, 2, 256, 256),
            pltpu.SemaphoreType.DMA((N_SEMS,)),
            pltpu.SemaphoreType.DMA((N_SEMS,)),
            pltpu.SemaphoreType.DMA,
            pltpu.SemaphoreType.DMA,
        ],
        compiler_params=pltpu.CompilerParams(
            collective_id=0, has_side_effects=True, vmem_limit_bytes=VMEM_BYTES
        ),
        cost_estimate=pl.CostEstimate(
            flops=flops, bytes_accessed=12 * 1024 * 1024, transcendentals=0
        ),
        name="adapt",
    )(hidden, weight, generators, cotangent)


def reduce_kernel(scale, n, parts, out, rbuf, sbuf, obuf, abuf, s1, r1, s2, r2):
    me = lax.axis_index("dp")
    barrier = pltpu.get_barrier_semaphore()
    for d in range(1, n):
        pl.semaphore_signal(
            barrier, inc=1, device_id={"dp": lax.rem(me + d, n)}, device_id_type=MESH
        )
    sbuf[...] = parts[...].astype(BF16)
    pl.semaphore_wait(barrier, n - 1)
    first = []
    for d in range(1, n):
        dev = lax.rem(me + d, n)
        c = pltpu.make_async_remote_copy(
            src_ref=sbuf.at[dev], dst_ref=rbuf.at[d], send_sem=s1.at[d], recv_sem=r1.at[d],
            device_id={"dp": dev}, device_id_type=MESH,
        )
        c.start()
        first.append(c)
    total = parts[me]
    for c, d in zip(first, range(1, n)):
        c.wait_recv()
        total = total + rbuf[d].astype(F32)
    obuf[...] = total * scale
    second = []
    for d in range(1, n):
        c = pltpu.make_async_remote_copy(
            src_ref=obuf, dst_ref=abuf.at[me], send_sem=s2.at[d], recv_sem=r2.at[d],
            device_id={"dp": lax.rem(me + d, n)}, device_id_type=MESH,
        )
        c.start()
        second.append(c)
    abuf[me] = obuf[...]
    for c in second:
        c.wait_recv()
    for pair in range(4):
        for c in range(4):
            for j in range(2):
                out[2 * pair + j, :, c * LANES : (c + 1) * LANES] = abuf[
                    pair * 4 + c, j * 64 : (j + 1) * 64
                ]
    for c in first + second:
        c.wait_send()


def reduce_call(parts, scale, n):
    return pl.pallas_call(
        functools.partial(reduce_kernel, scale, n),
        out_shape=jax.ShapeDtypeStruct((8, 64, 512), F32),
        in_specs=[pl.BlockSpec(memory_space=pltpu.VMEM)],
        out_specs=pl.BlockSpec(memory_space=pltpu.VMEM),
        scratch_shapes=[
            pltpu.VMEM((n, 128, 128), BF16),
            pltpu.VMEM((16, 128, 128), BF16),
            pltpu.VMEM((128, 128), F32),
            pltpu.VMEM((16, 128, 128), F32),
            pltpu.SemaphoreType.DMA((n,)),
            pltpu.SemaphoreType.DMA((n,)),
            pltpu.SemaphoreType.DMA((n,)),
            pltpu.SemaphoreType.DMA((n,)),
        ],
        compiler_params=pltpu.CompilerParams(
            collective_id=1, has_side_effects=True, vmem_limit_bytes=16 * 1024 * 1024
        ),
        name="dp_sum",
    )(parts)


def on_device(hidden, base_weight, generators, cotangent):
    n = lax.axis_size("dp")
    query, input_grad, parts = main_call(hidden, base_weight, generators, cotangent)
    scale = 1.0 / math.sqrt(hidden.shape[0] * n)
    return query, input_grad, reduce_call(parts, scale, n)


def solution(mesh):
    placed = (P("dp", "tensor"), P(None, "tensor"), P(None, None, "tensor"), P("dp", "tensor"))
    return jax.shard_map(
        on_device,
        mesh=mesh,
        in_specs=placed,
        out_specs=(P("dp", "tensor"), P("dp", "tensor"), P(None, None, "tensor")),
        check_vma=False,
    )
```

time: 680 us -> 194 us (0.29); the launches traced: 669 us -> 193 us
  waiting for transfers between devices: 405 us -> 0 us
  Pallas kernels: 0 us -> 187 us
  matrix products: 119 us -> 0 us
  local copies, waits for them, and re-layouts: 62.6 us -> 5.72 us
  other arithmetic: 35.6 us -> 0 us
  starting transfers between devices: 32.4 us -> 0 us
  between operations: 14.8 us -> 0.66 us
    pallas_call x0 -> x2, Pallas kernels: none -> 187 us  [the longest x1 155 us: main_call(): pl.pallas_call(main_kernel, out_shape=(jax.ShapeDtypeStruct((tokens, 512)...]
    reduce_scatter x1 -> x0, waiting for transfers between devices: 164 us -> none  [on_device(): lax.psum_scatter(lax.dot_general(weight_rows, base_grad_b, (((1,), (1,)),...]
    psum x1 -> x0, waiting for transfers between devices: 121 us -> none  [on_device(): factor_grad = lax.psum(stacked, 'dp') * (1.0 / math.sqrt(token_total))]
    dot_general x50 -> x0, matrix products: 119 us -> none  [the longest x8 17.3 us: mix_backward(): jnp.einsum('nci,ncr->icr', low_half, grad_out, precision=lax.Precision.HI...]
    ppermute x8 -> x0, waiting for transfers between devices: 119 us -> none  [from_partner(): return lax.ppermute(value, axis, pairs)]
    ppermute x8 -> x0, starting transfers between devices: 32.2 us -> none  [from_partner(): return lax.ppermute(value, axis, pairs)]
    slice x17 -> x0, local copies, waits for them, and re-layouts: 23.5 us -> none  [the longest x9 12.4 us: apply_mix(): factor[:half_block]]
    rev x8 -> x0, local copies, waits for them, and re-layouts: 16.9 us -> none  [pair_flip(): return shaped[:, :, ::-1].reshape(count, groups, half_block)]
  transfers between devices with their start and end apart: 11 -> 0, of which waited for: 9 -> 0; matrix products, arithmetic and copies ran while one was open for 19% -> 0% of each run, Pallas kernels for 0% -> 0%
where the time goes in v1:
time: 194 us; the launch traced here: 193 us
  Pallas kernels  187 us (96%)
  local copies, waits for them, and re-layouts  5.72 us (3%)
    pallas_call x1, Pallas kernels, main_call(): pl.pallas_call(main_kernel, out_shape=(jax.ShapeDtypeStruct((tokens, 512)...  155 us
    pallas_call x1, Pallas kernels, reduce_call(): pl.pallas_call(functools.partial(reduce_kernel, scale, n), out_shape=jax....  32.1 us
    unnamed x5, local copies, waits for them, and re-layouts  5.72 us

profile of v1, /device:TPU:1, one launch (start us, length us, event | category | flops | bytes accessed | tf_op | source)
XLA Modules:
  0.0 193.4 jit_solution(9507475530101211818)
XLA Ops:
  0.6 155.0 %adapt.1 = (bf16[384,512]{1,0:T(8,128)(2,1)}, bf16[384,512]{1,0:T(8,128)(2,1)}, f32[16,128,128]{2,1,0:T(8,128)}) custom-call(bf16[384,512]{1,0:T(8,128)(2,1)} %hid.1, bf16[8192,512]{1,0:T(8,128)(2,1)} %wt.1, f32[8,64,512]{2,1,0:T(8,128)} %gen.1, bf16[384,512]{1,0:T(8,128)(2,1)} %cot.1), custom_call_target="tpu_custom_call" | custom-call | flops 6442450944 | bytes 12582912 | tf_op jit(solution)/shard_map/adapt/pallas_call | solution.py:520
  155.6 0.0 copy-start
  155.6 1.2 copy-done
  156.8 32.1 %dp_sum.1 = f32[8,64,512]{2,1,0:T(8,128)S(1)} custom-call(f32[16,128,128]{2,1,0:T(8,128)S(1)} %copy-done), custom_call_target="tpu_custom_call" | custom-call | tf_op jit(solution)/shard_map/dp_sum/pallas_call | solution.py:614
  188.9 1.8 copy.10
  190.7 1.8 copy.11
  192.4 1.0 copy.12
Async XLA Ops:
  155.6 1.2 copy-start

commit v2 on v0

v2 whole, which is shorter than its diff:
```python
import functools
import math

import jax
import jax.numpy as jnp
from jax import lax
from jax.experimental import pallas as pl
from jax.experimental.pallas import tpu as pltpu
from jax.sharding import PartitionSpec as P

MESH = pl.DeviceIdType.MESH
F32 = jnp.float32
BF16 = jnp.bfloat16
SIDE = 4
LANES = 128
HALF = 32
VMEM_BYTES = 60 * 1024 * 1024


def wrap(value, n):
    return lax.rem(value + n, n)


def dot(a, b):
    return jnp.dot(a, b, preferred_element_type=F32)


def dot_nt(a, b):
    return lax.dot_general(a, b, (((1,), (1,)), ((), ())), preferred_element_type=F32)


def dot_tn(a, b):
    return lax.dot_general(a, b, (((0,), (0,)), ((), ())), preferred_element_type=F32)


def split(value):
    high = value.astype(BF16)
    return high, (value - high.astype(F32)).astype(BF16)


def put_split(ref, index, value):
    ref[(*index, 0)], ref[(*index, 1)] = split(value)


def mix(product, value, ref, index):
    top, rest = ref[(*index, 0)], ref[(*index, 1)]
    if value.dtype == BF16:
        return product(value, top) + product(value, rest)
    high, low = split(value)
    return product(high, top) + product(low, top) + product(high, rest)


def groups_of(shape):
    rows = lax.broadcasted_iota(jnp.int32, shape, 0) >> 5
    cols = lax.broadcasted_iota(jnp.int32, shape, 1) >> 5
    return rows, cols


def spread(block, mask, copies):
    return jnp.where(mask, jnp.concatenate([block] * copies, axis=0), 0.0)


def pair_matrix(gen_a, gen_b):
    both = jnp.concatenate([gen_a, gen_b], axis=1)
    rows, cols = groups_of((LANES, 2 * LANES))
    mask = rows == (cols & 3)
    return jnp.concatenate([spread(both[:HALF], mask, 4), spread(both[HALF:], mask, 4)], axis=0)


def pair_extract(grad):
    cols = (lax.broadcasted_iota(jnp.int32, (HALF, 2 * LANES), 1) >> 5) & 3
    parts = []
    for h in range(2):
        total = jnp.zeros((HALF, 2 * LANES), F32)
        for g in range(4):
            start = h * LANES + g * HALF
            total = total + jnp.where(cols == g, grad[start : start + HALF], 0.0)
        parts.append(total)
    return jnp.concatenate(parts, axis=0)


def near_matrix(gen, k):
    rows, cols = groups_of((256, 256))
    low = cols & ~(1 << k)
    return spread(gen[:HALF], rows == low, 8) + spread(gen[HALF:], rows == (low | (1 << k)), 8)


def near_extract(grad, k):
    cols = lax.broadcasted_iota(jnp.int32, (HALF, 256), 1) >> 5
    low = cols & ~(1 << k)
    parts = []
    for want in (low, low | (1 << k)):
        total = jnp.zeros((HALF, 256), F32)
        for g in range(8):
            total = total + jnp.where(want == g, grad[g * HALF : (g + 1) * HALF], 0.0)
        parts.append(total)
    return jnp.concatenate(parts, axis=0)


def diag_matrix(block):
    rows, cols = groups_of((256, 256))
    return spread(block, rows == cols, 8)


def diag_extract(grad):
    cols = lax.broadcasted_iota(jnp.int32, (HALF, 256), 1) >> 5
    total = jnp.zeros((HALF, 256), F32)
    for g in range(8):
        total = total + jnp.where(cols == g, grad[g * HALF : (g + 1) * HALF], 0.0)
    return total


PAIRS = (((0, 1), (2, 3)), ((0, 2), (1, 3)))
N_SEMS = 224
SPLIT_GATHER = 320
SPLIT_SUM = 320
STOP = None


class Stop(Exception):
    pass


class Sent:
    def __init__(self, copy):
        self.copy, self.received = copy, False

    def arrive(self):
        if not self.received:
            self.copy.wait_recv()
            self.received = True


def main_kernel(n_dp, scale, *refs):
    pending, endings = [], []
    try:
        main_body(n_dp, scale, pending, endings, *refs)
    except Stop:
        pass
    for c in pending:
        c.arrive()
        c.copy.wait_send()
    for end in endings:
        end()


def main_body(
    n_dp, scale, pending, endings,
    hid, wt, gen, cot, query, igrad, ggrad,
    w_v, hbuf, base, pb, gz, gy, gyb, gzb, ghome, gsave_y, gsave_z, glocal, slocal,
    szb, ssend, syb, qsend, qb, s5b, s7b, zsend, gsend_t, gsend_z, gb,
    rs_s2, rs_r2, rs_s1, rs_s3, rs_r1, rs_r3, q_s2, q_r2, q_s1, q_s3, q_r1, q_r3,
    gp, gp_z, gp_y, gpb, sums_a, sums_b, slab_a, slab_b, gout, mats_loc, mats_z, mats_y,
    send_sem, recv_sem, w_sem,
):
    tokens = hid.shape[0]
    me = lax.axis_index("tensor")
    my_dp = lax.axis_index("dp")
    y, z = me // SIDE, lax.rem(me, SIDE)
    z_of = lax.rem(y + z, SIDE)
    counter = [0]

    def mark(name):
        if STOP == name:
            raise Stop

    def at(dy, dz):
        return wrap(y + dy, SIDE) * SIDE + wrap(z + dz, SIDE)

    def toward(axis, step):
        return at(step, 0) if axis == "y" else at(0, step)

    def place(axis, step, fixed):
        return (step, fixed) if axis == "y" else (fixed, step)

    def ids(n=1):
        first = counter[0]
        counter[0] += n
        return first

    def copy(src, dst, send_index, recv_index, device):
        return pltpu.make_async_remote_copy(
            src_ref=src,
            dst_ref=dst,
            send_sem=send_sem.at[send_index],
            recv_sem=recv_sem.at[recv_index],
            device_id=device,
            device_id_type=MESH,
        )

    def send(src, dst, dev, axis="tensor"):
        index = ids()
        c = copy(src, dst, index, index, {axis: dev})
        c.start()
        c = Sent(c)
        pending.append(c)
        return c

    def w_rows(dy, dz):
        return w_v[pl.ds(pl.multiple_of(at(dy, dz) * 512, 512), 512), :]

    def chunk_at(index):
        return pl.ds(pl.multiple_of(index * LANES, LANES), LANES)

    w_copy = pltpu.make_async_copy(wt, w_v, w_sem)
    w_copy.start()

    barrier = pltpu.get_barrier_semaphore()
    for d in range(1, 16):
        pl.semaphore_signal(
            barrier, inc=1, device_id={"tensor": lax.rem(me + d, 16)}, device_id_type=MESH
        )
    for d in range(1, n_dp):
        pl.semaphore_signal(
            barrier, inc=1, device_id={"dp": lax.rem(my_dp + d, n_dp)}, device_id_type=MESH
        )
    pl.semaphore_wait(barrier, 15 + n_dp - 1)

    cot_in, genz_in, geny_in = [], [], []
    for d in range(1, 4):
        cols = chunk_at(lax.rem(y + d + z, SIDE))
        cot_in.append(send(cot.at[:, cols], gyb.at[y], at(d, 0)))
        geny_in.append(send(gen.at[pl.ds(6, 2), :, cols], gy.at[y], at(d, 0)))

    def held(dy, dz, lo, hi):
        ref = hid if (dy, dz) == (0, 0) else hbuf.at[dy, dz]
        return ref.at[pl.ds(lo, hi - lo)]

    arrivals = {(dy, dz): [] for dy in range(4) for dz in range(4)}

    def hop(axis, fixed, step, sign, lo, hi):
        target = place(axis, step + sign & 3, fixed)
        c = send(
            held(*place(axis, step, fixed), lo, hi),
            hbuf.at[(*target, pl.ds(lo, hi - lo))],
            toward(axis, sign),
        )
        arrivals[target].append(c)
        return c

    def ring_start(axis, fixed, lo, hi):
        return [hop(axis, fixed, 0, 1, lo, hi), hop(axis, fixed, 0, -1, lo, hi)]

    def ring_forward(axis, fixed, lo, hi, copies):
        middle = (lo + hi) // 2
        copies[0].arrive()
        copies.append(hop(axis, fixed, 1, 1, lo, middle))
        copies[1].arrive()
        copies.append(hop(axis, fixed, 3, -1, middle, hi))

    cut = SPLIT_GATHER * tokens // 384 // 32 * 32
    routes = [("z", "y", 0, cut)]
    if cut < tokens:
        routes.append(("y", "z", cut, tokens))
    first = [ring_start(a, 0, lo, hi) for a, _, lo, hi in routes]
    second = [{0: ring_start(b, 0, lo, hi)} for _, b, lo, hi in routes]
    for d in range(1, 4):
        cols = chunk_at(wrap(z + d, SIDE))
        genz_in.append(send(gen.at[pl.ds(4, 2), :, cols], gz.at[z], at(0, d)))

    def gather_second(step):
        for (_, b, lo, hi), copies in zip(routes, second):
            ring_forward(b, step, lo, hi, copies[step])

    def gather_first():
        for (a, b, lo, hi), ring, copies in zip(routes, first, second):
            middle = (lo + hi) // 2
            ring[0].arrive()
            ring.append(hop(a, 0, 1, 1, lo, middle))
            copies[1] = ring_start(b, 1, lo, hi)
            ring[1].arrive()
            ring.append(hop(a, 0, 3, -1, middle, hi))
            copies[3] = ring_start(b, 3, lo, hi)

    def gather_far():
        for (_, b, lo, hi), ring, copies in zip(routes, first, second):
            ring[2].arrive()
            ring[3].arrive()
            copies[2] = ring_start(b, 2, lo, hi)

    def accumulate(*blocks):
        for dy, dz in blocks:
            for c in arrivals[dy, dz]:
                c.arrive()
            base[...] += dot(hbuf[dy, dz], w_rows(-dy, -dz))

    gyb[y] = cot[:, chunk_at(z_of)]
    gy[y] = gen[6:8, :, chunk_at(z_of)]
    gz[z] = gen[4:6, :, chunk_at(z)]

    for k in range(3):
        for s in range(2):
            put_split(mats_loc, (k, s), near_matrix(gen[k, :, 256 * s : 256 * s + 256], k))
    for s in range(2):
        for h in range(2):
            block = gen[3, HALF * h : HALF * h + HALF, 256 * s : 256 * s + 256]
            put_split(mats_loc, (3 + h, s), diag_matrix(block))

    def pair_of(ref, a, b):
        return jnp.concatenate([ref[a], ref[b]], axis=1)

    def fill_pairs(mats, gens):
        for k in range(2):
            for i, (a, b) in enumerate(PAIRS[k]):
                put_split(mats, (k, i), pair_matrix(gens[a, k], gens[b, k]))

    def pairs_apply(product, order, source, mats, save, out):
        values = None
        for k, target in zip(order, (save, out)):
            new = [None] * 4
            for i, (a, b) in enumerate(PAIRS[k]):
                if values is None:
                    v = pair_of(source, a, b)
                else:
                    v = jnp.concatenate([values[a], values[b]], axis=1)
                v = v.astype(F32) + mix(product, v, mats, (k, i))
                new[a], new[b] = v[:, :LANES], v[:, LANES:]
            values = new
            for m in range(4):
                target[m] = values[m].astype(BF16)

    def cross(src, dst, own_slot, dev_of, src_of):
        index = ids(4)
        sent = []
        for d in range(4):
            c = copy(
                src.at[src_of(d)], dst.at[own_slot], index + d, index + own_slot,
                {"tensor": dev_of(d)},
            )
            if d == 0:
                keep = pltpu.make_async_copy(
                    src.at[src_of(0)], dst.at[own_slot], recv_sem.at[index + own_slot]
                )
                pl.when(dev_of(0) != me)(lambda c=c: c.start())
                pl.when(dev_of(0) == me)(lambda keep=keep: keep.start())
            else:
                c.start()
            sent.append(c)
        done = []

        def arrive():
            if not done:
                done.append(True)
                for m in range(4):
                    pltpu.make_async_copy(src.at[m], dst.at[m], recv_sem.at[index + m]).wait()

        def finish():
            arrive()
            pl.when(dev_of(0) != me)(lambda: sent[0].wait_send())
            for c in sent[1:]:
                c.wait_send()

        endings.append(finish)
        return arrive

    for c in geny_in:
        c.arrive()
    fill_pairs(mats_y, gy)
    for c in cot_in:
        c.arrive()
    pairs_apply(dot_nt, (1, 0), gyb, mats_y, gsave_y, gsend_t)
    bwd_arrive = cross(
        gsend_t, gzb, z,
        lambda d: wrap(y + d, SIDE) * SIDE + z_of,
        lambda d: wrap(y + d, SIDE),
    )
    mark("bwd_y")

    w_copy.wait()
    base[...] = dot(hid[...], w_rows(0, 0))
    gather_second(0)
    for c in genz_in:
        c.arrive()
    fill_pairs(mats_z, gz)
    mark("ag0")

    gather_first()
    accumulate((1, 0), (3, 0), (0, 1), (0, 3))
    mark("ag1")

    bwd_arrive()
    pairs_apply(dot_nt, (1, 0), gzb, mats_z, gsave_z, gsend_z)
    back_in = []
    for d in range(1, 4):
        back_in.append(send(gsend_z.at[wrap(z + d, SIDE)], ghome.at[z], at(0, d)))
    ghome[z] = gsend_z[z]
    mark("bwd_z")

    gather_far()
    accumulate((2, 0), (0, 2))
    gather_second(1)
    accumulate((1, 1), (3, 1))
    mark("ag2")

    for c in back_in:
        c.arrive()
    ga = pair_of(ghome, 0, 1)
    gc = pair_of(ghome, 2, 3)
    glocal[3, 0], glocal[3, 1] = ga, gc
    fa = ga.astype(F32) + mix(dot_nt, ga, mats_loc, (3, 0)) + mix(dot_nt, gc, mats_loc, (3, 1))
    fb = gc.astype(F32) + mix(dot_nt, ga, mats_loc, (4, 0)) + mix(dot_nt, gc, mats_loc, (4, 1))
    for k in (2, 1, 0):
        glocal[k, 0], glocal[k, 1] = fa.astype(BF16), fb.astype(BF16)
        fa = fa + mix(dot_nt, fa, mats_loc, (k, 0))
        fb = fb + mix(dot_nt, fb, mats_loc, (k, 1))
    gb[:, :256] = fa.astype(BF16)
    gb[:, 256:] = fb.astype(BF16)
    mark("bwd_local")

    gather_second(3)
    accumulate((1, 3), (3, 3))
    gather_second(2)
    accumulate((1, 2), (3, 2))
    mark("ag3")

    computed = set()

    def partial(dy, dz, lo, hi):
        if (dy, dz) not in computed:
            computed.add((dy, dz))
            pb[dy, dz] = dot_nt(gb[...], w_rows(dy, dz))
        return pb[dy, dz, lo:hi]

    class Sum:
        def __init__(self, a, b, lo, hi):
            self.a, self.b, self.lo, self.hi, self.middle = a, b, lo, hi, (lo + hi) // 2
            self.copies, self.last = {}, []
            self.rows = pl.ds(lo, hi - lo)
            self.top, self.low = pl.ds(lo, self.middle - lo), pl.ds(self.middle, hi - self.middle)

        def far(self, fixed):
            block = partial(*place(self.a, 2, fixed), self.lo, self.hi)
            rs_s2[fixed, self.rows] = block.astype(BF16)
            self.copies[fixed] = [
                send(rs_s2.at[fixed, self.top], rs_r2.at[fixed, self.top], toward(self.a, 1)),
                send(rs_s2.at[fixed, self.low], rs_r2.at[fixed, self.low], toward(self.a, -1)),
            ]

        def near(self, fixed):
            cs, size = self.copies[fixed], self.middle - self.lo
            p = partial(*place(self.a, 1, fixed), self.lo, self.hi)
            cs[0].arrive()
            rs_s1[fixed, self.top] = (p[:size] + rs_r2[fixed, self.top].astype(F32)).astype(BF16)
            rs_s1[fixed, self.low] = p[size:].astype(BF16)
            cs.append(
                send(rs_s1.at[fixed, self.rows], rs_r1.at[fixed, self.rows], toward(self.a, 1))
            )
            p = partial(*place(self.a, 3, fixed), self.lo, self.hi)
            cs[1].arrive()
            rs_s3[fixed, self.top] = p[:size].astype(BF16)
            rs_s3[fixed, self.low] = (p[size:] + rs_r2[fixed, self.low].astype(F32)).astype(BF16)
            cs.append(
                send(rs_s3.at[fixed, self.rows], rs_r3.at[fixed, self.rows], toward(self.a, -1))
            )

        def whole(self, fixed):
            p = partial(*place(self.a, 0, fixed), self.lo, self.hi)
            for c in self.copies[fixed][2:]:
                c.arrive()
            return p + rs_r1[fixed, self.rows].astype(F32) + rs_r3[fixed, self.rows].astype(F32)

        def last_far(self):
            q_s2[self.rows] = self.whole(2).astype(BF16)
            self.last = [
                send(q_s2.at[self.top], q_r2.at[self.top], toward(self.b, 1)),
                send(q_s2.at[self.low], q_r2.at[self.low], toward(self.b, -1)),
            ]

        def last_near(self):
            size = self.middle - self.lo
            q = self.whole(1)
            self.last[0].arrive()
            q_s1[self.top] = (q[:size] + q_r2[self.top].astype(F32)).astype(BF16)
            q_s1[self.low] = q[size:].astype(BF16)
            self.last.append(send(q_s1.at[self.rows], q_r1.at[self.rows], toward(self.b, 1)))
            q = self.whole(3)
            self.last[1].arrive()
            q_s3[self.top] = q[:size].astype(BF16)
            q_s3[self.low] = (q[size:] + q_r2[self.low].astype(F32)).astype(BF16)
            self.last.append(send(q_s3.at[self.rows], q_r3.at[self.rows], toward(self.b, -1)))

        def end(self):
            q = self.whole(0)
            for c in self.last[2:]:
                c.arrive()
            q = q + q_r1[self.rows].astype(F32) + q_r3[self.rows].astype(F32)
            igrad[self.rows] = q.astype(BF16)

    cut = SPLIT_SUM * tokens // 384 // 32 * 32
    sums = [Sum("y", "z", 0, cut)]
    if cut < tokens:
        sums.append(Sum("z", "y", cut, tokens))
    for fixed in (2, 1, 3, 0):
        for s in sums:
            s.far(fixed)
    mark("rs_far")

    accumulate((2, 1), (2, 3), (2, 2))
    mark("base")
    fa, fb = base[:, :256], base[:, 256:]
    for k in range(3):
        slocal[k, 0], slocal[k, 1] = fa.astype(BF16), fb.astype(BF16)
        fa = fa + mix(dot, fa, mats_loc, (k, 0))
        fb = fb + mix(dot, fb, mats_loc, (k, 1))
    slocal[3, 0], slocal[3, 1] = fa.astype(BF16), fb.astype(BF16)
    fc = fa + mix(dot, fa, mats_loc, (3, 0)) + mix(dot, fb, mats_loc, (4, 0))
    fd = fb + mix(dot, fa, mats_loc, (3, 1)) + mix(dot, fb, mats_loc, (4, 1))
    for c in range(4):
        side = fc if c < 2 else fd
        ssend[c] = side[:, (c % 2) * LANES : (c % 2) * LANES + LANES].astype(BF16)
    fwd_in = []
    for d in range(1, 4):
        fwd_in.append(send(ssend.at[wrap(z + d, SIDE)], szb.at[z], at(0, d)))
    szb[z] = ssend[z]
    mark("fwd_local")

    for fixed in (2, 1):
        for s in sums:
            s.near(fixed)
    mark("near1")

    def put_local(k, s, value):
        for j in range(2):
            gp[pl.ds(((k // 2) * 4 + 2 * s + j) * 128 + (k % 2) * 64, 64)] = value[
                :, j * LANES : (j + 1) * LANES
            ]

    for k in range(3):
        for s in range(2):
            put_local(k, s, near_extract(dot_tn(slocal[k, s], glocal[k, s]), k))
    for s in range(2):
        put_local(
            3, s,
            jnp.concatenate(
                [diag_extract(dot_tn(slocal[3, h], glocal[3, s])) for h in range(2)], axis=0
            ),
        )

    for c in fwd_in:
        c.arrive()
    pairs_apply(dot, (0, 1), szb, mats_z, s5b, zsend)
    fwd_arrive = cross(
        zsend, syb, y,
        lambda d: ((SIDE - d) % SIDE) * SIDE + wrap(z + d, SIDE),
        lambda d: wrap(z + d, SIDE),
    )
    mark("fwd_z")

    def pair_grads(states, grads, dst):
        for k in range(2):
            for i, (a, b) in enumerate(PAIRS[k]):
                value = pair_extract(dot_tn(pair_of(states[k], a, b), pair_of(grads[k], a, b)))
                dst[a, k * 64 : k * 64 + 64] = value[:, :LANES]
                dst[b, k * 64 : k * 64 + 64] = value[:, LANES:]

    def piece(index):
        return pl.ds(pl.multiple_of(index * 128, 128), 128)

    pair_grads((szb, s5b), (gsave_z, gzb), gp_z)
    outz_in = []
    for d in range(1, 4):
        outz_in.append(send(gp_z.at[wrap(z + d, SIDE)], gp.at[piece(8 + z)], at(0, d)))
    gp[piece(8 + z)] = gp_z[z]

    for fixed in (3, 0):
        for s in sums:
            s.near(fixed)
    mark("near2")

    fwd_arrive()
    pairs_apply(dot, (0, 1), syb, mats_y, s7b, qsend)
    query_in = []
    for d in range(1, 4):
        query_in.append(send(qsend.at[wrap(y + d, SIDE)], qb.at[z_of], at(d, 0)))
    qb[z_of] = qsend[y]
    mark("fwd_y")

    pair_grads((syb, s7b), (gsave_y, gyb), gp_y)
    outy_in = []
    for d in range(1, 4):
        outy_in.append(send(gp_y.at[wrap(y + d, SIDE)], gp.at[piece(12 + z_of)], at(d, 0)))
    gp[piece(12 + z_of)] = gp_y[y]
    mark("grads")

    class Slabs:
        def __init__(self, start, size, sums_ref, slab_ref):
            self.start, self.size = start, size
            self.sums_ref, self.slab_ref = sums_ref, slab_ref
            self.ins, self.outs = [], []

        def rows(self, dev):
            return pl.ds(pl.multiple_of(self.start + dev * self.size, 32), self.size)

        def scatter(self):
            all_rows = pl.ds(self.start, 16 * self.size)
            gpb[all_rows] = gp[all_rows].astype(BF16)
            for d in range(1, n_dp):
                dev = lax.rem(my_dp + d, n_dp)
                self.ins.append(send(gpb.at[self.rows(dev)], self.sums_ref.at[d], dev, "dp"))

        def gather(self):
            total = gp[self.rows(my_dp)]
            for d, c in zip(range(1, n_dp), self.ins):
                c.arrive()
                total = total + self.sums_ref[d].astype(F32)
            self.slab_ref[...] = total * scale
            for d in range(1, n_dp):
                dev = lax.rem(my_dp + d, n_dp)
                self.outs.append(send(self.slab_ref, gout.at[self.rows(my_dp)], dev, "dp"))
            gout[self.rows(my_dp)] = self.slab_ref[...]

        def finish(self):
            for c in self.outs:
                c.arrive()

    early, late = Slabs(0, 96, sums_a, slab_a), Slabs(1536, 32, sums_b, slab_b)
    for c in outz_in:
        c.arrive()
    if n_dp > 1:
        early.scatter()

    for s in sums:
        s.last_far()
    mark("last_far")
    for c in outy_in:
        c.arrive()
    if n_dp > 1:
        late.scatter()
        early.gather()
    for s in sums:
        s.last_near()
    mark("last_near")
    if n_dp > 1:
        late.gather()

    for c in query_in:
        c.arrive()
    for c in range(4):
        query[:, c * LANES : (c + 1) * LANES] = qb[c]
    mark("query")
    for s in sums:
        s.end()
    mark("igrad")
    if n_dp > 1:
        early.finish()
        late.finish()
    final = gout if n_dp > 1 else gp
    for pair in range(4):
        for c in range(4):
            for j in range(2):
                ggrad[2 * pair + j, :, c * LANES : (c + 1) * LANES] = final[
                    pl.ds((pair * 4 + c) * 128 + j * 64, 64)
                ]


def main_call(hidden, weight, generators, cotangent, n_dp=1, scale=1.0):
    tokens = hidden.shape[0]
    vm = lambda *shape, dtype=BF16: pltpu.VMEM(shape, dtype)
    chunks = vm(4, tokens, LANES)
    block = vm(tokens, 512)
    blocks = vm(4, tokens, 512)
    flops = 4 * tokens * 8192 * 512
    return pl.pallas_call(
        functools.partial(main_kernel, n_dp, scale),
        out_shape=(
            jax.ShapeDtypeStruct((tokens, 512), BF16),
            jax.ShapeDtypeStruct((tokens, 512), BF16),
            jax.ShapeDtypeStruct((8, 64, 512), F32),
        ),
        in_specs=[
            pl.BlockSpec(memory_space=pltpu.VMEM),
            pl.BlockSpec(memory_space=pl.ANY),
            pl.BlockSpec(memory_space=pltpu.VMEM),
            pl.BlockSpec(memory_space=pltpu.VMEM),
        ],
        out_specs=[pl.BlockSpec(memory_space=pltpu.VMEM)] * 3,
        scratch_shapes=[
            vm(8192, 512),
            vm(4, 4, tokens, 512),
            vm(tokens, 512, dtype=F32),
            vm(4, 4, tokens, 512, dtype=F32),
            vm(4, 2, 64, LANES, dtype=F32),
            vm(4, 2, 64, LANES, dtype=F32),
            chunks, chunks, chunks, chunks, chunks,
            vm(4, 2, tokens, 256),
            vm(4, 2, tokens, 256),
            chunks, chunks, chunks, chunks, chunks,
            chunks, chunks, chunks, chunks, chunks,
            block,
            blocks, blocks, blocks, blocks, blocks, blocks,
            block, block, block, block, block, block,
            vm(2048, 128, dtype=F32),
            vm(4, 128, 128, dtype=F32),
            vm(4, 128, 128, dtype=F32),
            vm(2048, 128),
            vm(16, 96, 128),
            vm(16, 32, 128),
            vm(96, 128, dtype=F32),
            vm(32, 128, dtype=F32),
            vm(2048, 128, dtype=F32),
            vm(5, 2, 2, 256, 256),
            vm(2, 2, 2, 256, 256),
            vm(2, 2, 2, 256, 256),
            pltpu.SemaphoreType.DMA((N_SEMS,)),
            pltpu.SemaphoreType.DMA((N_SEMS,)),
            pltpu.SemaphoreType.DMA,
        ],
        compiler_params=pltpu.CompilerParams(
            collective_id=0, has_side_effects=True, vmem_limit_bytes=VMEM_BYTES
        ),
        cost_estimate=pl.CostEstimate(
            flops=flops, bytes_accessed=12 * 1024 * 1024, transcendentals=0
        ),
        name="adapt",
    )(hidden, weight, generators, cotangent)


def copy_kernel(*refs):
    count = len(refs) // 2
    sems = refs[-1]
    copies = [
        pltpu.make_async_copy(refs[i], refs[count + i], sems.at[i]) for i in range(count)
    ]
    for c in copies:
        c.start()
    for c in copies:
        c.wait()


def copy_call(*arrays):
    anywhere = pl.BlockSpec(memory_space=pl.ANY)
    return pl.pallas_call(
        copy_kernel,
        out_shape=tuple(jax.ShapeDtypeStruct(a.shape, a.dtype) for a in arrays),
        in_specs=[anywhere] * len(arrays),
        out_specs=[anywhere] * len(arrays),
        scratch_shapes=[pltpu.SemaphoreType.DMA((len(arrays),))],
        name="results",
    )(*arrays)


def on_device(hidden, base_weight, generators, cotangent):
    n = lax.axis_size("dp")
    scale = 1.0 / math.sqrt(hidden.shape[0] * n)
    return copy_call(*main_call(hidden, base_weight, generators, cotangent, n, scale))


def solution(mesh):
    placed = (P("dp", "tensor"), P(None, "tensor"), P(None, None, "tensor"), P("dp", "tensor"))
    return jax.shard_map(
        on_device,
        mesh=mesh,
        in_specs=placed,
        out_specs=(P("dp", "tensor"), P("dp", "tensor"), P(None, None, "tensor")),
        check_vma=False,
    )
```

time: 680 us -> 235 us (0.35); the launches traced: 669 us -> 234 us
  waiting for transfers between devices: 405 us -> 0 us
  Pallas kernels: 0 us -> 233 us
  matrix products: 119 us -> 0 us
  local copies, waits for them, and re-layouts: 62.6 us -> 0 us
  other arithmetic: 35.6 us -> 0 us
  starting transfers between devices: 32.4 us -> 0 us
  between operations: 14.8 us -> 0.8 us
    pallas_call x0 -> x2, Pallas kernels: none -> 233 us  [the longest x1 176 us: main_call(): pl.pallas_call(functools.partial(main_kernel, n_dp, scale), out_shape=(ja...]
    reduce_scatter x1 -> x0, waiting for transfers between devices: 164 us -> none  [on_device(): lax.psum_scatter(lax.dot_general(weight_rows, base_grad_b, (((1,), (1,)),...]
    psum x1 -> x0, waiting for transfers between devices: 121 us -> none  [on_device(): factor_grad = lax.psum(stacked, 'dp') * (1.0 / math.sqrt(token_total))]
    dot_general x50 -> x0, matrix products: 119 us -> none  [the longest x8 17.3 us: mix_backward(): jnp.einsum('nci,ncr->icr', low_half, grad_out, precision=lax.Precision.HI...]
    ppermute x8 -> x0, waiting for transfers between devices: 119 us -> none  [from_partner(): return lax.ppermute(value, axis, pairs)]
    ppermute x8 -> x0, starting transfers between devices: 32.2 us -> none  [from_partner(): return lax.ppermute(value, axis, pairs)]
    slice x17 -> x0, local copies, waits for them, and re-layouts: 23.5 us -> none  [the longest x9 12.4 us: apply_mix(): factor[:half_block]]
    rev x8 -> x0, local copies, waits for them, and re-layouts: 16.9 us -> none  [pair_flip(): return shaped[:, :, ::-1].reshape(count, groups, half_block)]
  transfers between devices with their start and end apart: 11 -> 0, of which waited for: 9 -> 0; matrix products, arithmetic and copies ran while one was open for 19% -> 0% of each run, Pallas kernels for 0% -> 0%
where the time goes in v2:
time: 235 us; the launch traced here: 234 us
  Pallas kernels  233 us (99%)
    pallas_call x1, Pallas kernels, main_call(): pl.pallas_call(functools.partial(main_kernel, n_dp, scale), out_shape=(ja...  176 us
    pallas_call x1, Pallas kernels, copy_call(): pl.pallas_call(copy_kernel, out_shape=tuple((jax.ShapeDtypeStruct(a.shape...  56.7 us

profile of v2, /device:TPU:1, one launch (start us, length us, event | category | flops | bytes accessed | tf_op | source)
XLA Modules:
  0.0 233.9 jit_solution(17534258617493499812)
XLA Ops:
  0.6 176.4 %adapt.1 = (bf16[384,512]{1,0:T(8,128)(2,1)}, bf16[384,512]{1,0:T(8,128)(2,1)}, f32[8,64,512]{2,1,0:T(8,128)}) custom-call(bf16[384,512]{1,0:T(8,128)(2,1)} %refs_0_.1, bf16[8192,512]{1,0:T(8,128)(2,1)} %refs_1_.1, f32[8,64,512]{2,1,0:T(8,128)} %refs_2_.1, bf16[384,512]{1,0:T(8,128)(2,1)} %refs_3_.1), custom_call_target="tpu_custom_call" | custom-call | flops 6442450944 | bytes 12582912 | tf_op jit(solution)/shard_map/adapt/pallas_call | solution.py:663
  177.1 56.7 %results.1 = (bf16[384,512]{1,0:T(8,128)(2,1)}, bf16[384,512]{1,0:T(8,128)(2,1)}, f32[8,64,512]{2,1,0:T(8,128)}) custom-call(bf16[384,512]{1,0:T(8,128)(2,1)} %get-tuple-element.6.refs_0_, bf16[384,512]{1,0:T(8,128)(2,1)} %get-tuple-element.7.refs_1_, f32[8,64,512]{2,1,0:T(8,128)} %get-tuple-element.8.refs_2_), custom_call_target="tpu_custom_call" | custom-call | tf_op jit(solution)/shard_map/results/pallas_call | solution.py:732

commit v3 on v2

--- a/solution.py
+++ b/solution.py
@@ -147,7 +147,7 @@
 def main_body(
     n_dp, scale, pending, endings,
     hid, wt, gen, cot, query, igrad, ggrad,
-    w_v, hbuf, base, pb, gz, gy, gyb, gzb, ghome, gsave_y, gsave_z, glocal, slocal,
+    w_v, hbuf, base, pb, gz, gy, gyb, gzb, ghome, gsave_y, gsave_z, gmid, glocal, slocal,
     szb, ssend, syb, qsend, qb, s5b, s7b, zsend, gsend_t, gsend_z, gb,
     rs_s2, rs_r2, rs_s1, rs_s3, rs_r1, rs_r3, q_s2, q_r2, q_s1, q_s3, q_r1, q_r3,
     gp, gp_z, gp_y, gpb, sums_a, sums_b, slab_a, slab_b, gout, mats_loc, mats_z, mats_y,
@@ -162,6 +162,8 @@
 
     def mark(name):
         if STOP == name:
+            if name == "bwd_y":
+                w_copy.wait()
             raise Stop
 
     def at(dy, dz):
@@ -359,26 +361,34 @@
     for c in cot_in:
         c.arrive()
     pairs_apply(dot_nt, (1, 0), gyb, mats_y, gsave_y, gsend_t)
-    bwd_arrive = cross(
-        gsend_t, gzb, z,
-        lambda d: wrap(y + d, SIDE) * SIDE + z_of,
-        lambda d: wrap(y + d, SIDE),
-    )
+    step_in = []
+    for d in range(1, 4):
+        step_in.append(send(gsend_t.at[wrap(y + d, SIDE)], gmid.at[z_of], at(d, 0)))
+    gmid[z_of] = gsend_t[y]
     mark("bwd_y")
 
+    gather_second(0)
+    for c in genz_in:
+        c.arrive()
+    fill_pairs(mats_z, gz)
+    for c in step_in:
+        c.arrive()
+    step_in = []
+    for d in range(1, 4):
+        step_in.append(send(gmid.at[wrap(z + d, SIDE)], gzb.at[z], at(0, d)))
+    gzb[z] = gmid[z]
     w_copy.wait()
     base[...] = dot(hid[...], w_rows(0, 0))
-    gather_second(0)
-    for c in genz_in:
-        c.arrive()
-    fill_pairs(mats_z, gz)
     mark("ag0")
 
     gather_first()
     accumulate((1, 0), (3, 0), (0, 1), (0, 3))
     mark("ag1")
-
-    bwd_arrive()
+    gather_far()
+    accumulate((2, 0), (0, 2))
+
+    for c in step_in:
+        c.arrive()
     pairs_apply(dot_nt, (1, 0), gzb, mats_z, gsave_z, gsend_z)
     back_in = []
     for d in range(1, 4):
@@ -386,10 +396,10 @@
     ghome[z] = gsend_z[z]
     mark("bwd_z")
 
-    gather_far()
-    accumulate((2, 0), (0, 2))
     gather_second(1)
     accumulate((1, 1), (3, 1))
+    gather_second(3)
+    accumulate((1, 3), (3, 3))
     mark("ag2")
 
     for c in back_in:
@@ -407,8 +417,6 @@
     gb[:, 256:] = fb.astype(BF16)
     mark("bwd_local")
 
-    gather_second(3)
-    accumulate((1, 3), (3, 3))
     gather_second(2)
     accumulate((1, 2), (3, 2))
     mark("ag3")
@@ -545,6 +553,12 @@
         lambda d: wrap(z + d, SIDE),
     )
     mark("fwd_z")
+    for fixed in (3, 0):
+        for s in sums:
+            s.near(fixed)
+    for s in sums:
+        s.last_far()
+    mark("near2")
 
     def pair_grads(states, grads, dst):
         for k in range(2):
@@ -561,11 +575,6 @@
     for d in range(1, 4):
         outz_in.append(send(gp_z.at[wrap(z + d, SIDE)], gp.at[piece(8 + z)], at(0, d)))
     gp[piece(8 + z)] = gp_z[z]
-
-    for fixed in (3, 0):
-        for s in sums:
-            s.near(fixed)
-    mark("near2")
 
     fwd_arrive()
     pairs_apply(dot, (0, 1), syb, mats_y, s7b, qsend)
@@ -613,25 +622,23 @@
             for c in self.outs:
                 c.arrive()
 
+    for s in sums:
+        s.last_near()
+    mark("last_near")
     early, late = Slabs(0, 96, sums_a, slab_a), Slabs(1536, 32, sums_b, slab_b)
     for c in outz_in:
         c.arrive()
     if n_dp > 1:
         early.scatter()
 
-    for s in sums:
-        s.last_far()
-    mark("last_far")
     for c in outy_in:
         c.arrive()
     if n_dp > 1:
         late.scatter()
         early.gather()
-    for s in sums:
-        s.last_near()
-    mark("last_near")
     if n_dp > 1:
         late.gather()
+    mark("dp")
 
     for c in query_in:
         c.arrive()
@@ -681,7 +688,7 @@
             vm(4, 4, tokens, 512, dtype=F32),
             vm(4, 2, 64, LANES, dtype=F32),
             vm(4, 2, 64, LANES, dtype=F32),
-            chunks, chunks, chunks, chunks, chunks,
+            chunks, chunks, chunks, chunks, chunks, chunks,
             vm(4, 2, tokens, 256),
             vm(4, 2, tokens, 256),
             chunks, chunks, chunks, chunks, chunks,
@@ -717,24 +724,17 @@
 
 def copy_kernel(*refs):
     count = len(refs) // 2
-    sems = refs[-1]
-    copies = [
-        pltpu.make_async_copy(refs[i], refs[count + i], sems.at[i]) for i in range(count)
-    ]
-    for c in copies:
-        c.start()
-    for c in copies:
-        c.wait()
+    for source, target in zip(refs[:count], refs[count:]):
+        target[...] = source[...]
 
 
 def copy_call(*arrays):
-    anywhere = pl.BlockSpec(memory_space=pl.ANY)
+    whole = pl.BlockSpec(memory_space=pltpu.VMEM)
     return pl.pallas_call(
         copy_kernel,
         out_shape=tuple(jax.ShapeDtypeStruct(a.shape, a.dtype) for a in arrays),
-        in_specs=[anywhere] * len(arrays),
-        out_specs=[anywhere] * len(arrays),
-        scratch_shapes=[pltpu.SemaphoreType.DMA((len(arrays),))],
+        in_specs=[whole] * len(arrays),
+        out_specs=[whole] * len(arrays),
         name="results",
     )(*arrays)
 

time: 235 us -> 170 us (0.72)
  Pallas kernels: 233 us -> 169 us
    pallas_call x1, Pallas kernels: 56.7 us -> 2.73 us  [copy_call(): pl.pallas_call(copy_kernel, out_shape=tuple((jax.ShapeDtypeStruct(a.shape...]
    pallas_call x1, Pallas kernels: 176 us -> 166 us  [main_call(): pl.pallas_call(functools.partial(main_kernel, n_dp, scale), out_shape=(ja...]
where the time goes in v3:
time: 170 us; the launch traced here: 169 us
  Pallas kernels  169 us (99%)
    pallas_call x1, Pallas kernels, main_call(): pl.pallas_call(functools.partial(main_kernel, n_dp, scale), out_shape=(ja...  166 us

profile of v3, /device:TPU:1, one launch (start us, length us, event | category | flops | bytes accessed | tf_op | source)
XLA Modules:
  0.0 169.1 jit_solution(8530561677368700511)
XLA Ops:
  0.6 165.8 %adapt.1 = (bf16[384,512]{1,0:T(8,128)(2,1)}, bf16[384,512]{1,0:T(8,128)(2,1)}, f32[8,64,512]{2,1,0:T(8,128)}) custom-call(bf16[384,512]{1,0:T(8,128)(2,1)} %refs_0_.1, bf16[8192,512]{1,0:T(8,128)(2,1)} %refs_1_.1, f32[8,64,512]{2,1,0:T(8,128)} %refs_2_.1, bf16[384,512]{1,0:T(8,128)(2,1)} %refs_3_.1), custom_call_target="tpu_custom_call" | custom-call | flops 6442450944 | bytes 12582912 | tf_op jit(solution)/shard_map/adapt/pallas_call | solution.py:670
  166.4 2.7 %results.1 = (bf16[384,512]{1,0:T(8,128)(2,1)}, bf16[384,512]{1,0:T(8,128)(2,1)}, f32[8,64,512]{2,1,0:T(8,128)}) custom-call(bf16[384,512]{1,0:T(8,128)(2,1)} %get-tuple-element.6.refs_0_, bf16[384,512]{1,0:T(8,128)(2,1)} %get-tuple-element.7.refs_1_, f32[8,64,512]{2,1,0:T(8,128)} %get-tuple-element.8.refs_2_), custom_call_target="tpu_custom_call" | custom-call | tf_op jit(solution)/shard_map/results/pallas_call | solution.py:733

commit v4 on v3

--- a/solution.py
+++ b/solution.py
@@ -112,8 +112,8 @@
 
 PAIRS = (((0, 1), (2, 3)), ((0, 2), (1, 3)))
 N_SEMS = 224
-SPLIT_GATHER = 320
-SPLIT_SUM = 320
+SPLIT_GATHER = 352
+SPLIT_SUM = 352
 STOP = None
 
 
@@ -147,17 +147,16 @@
 def main_body(
     n_dp, scale, pending, endings,
     hid, wt, gen, cot, query, igrad, ggrad,
-    w_v, hbuf, base, pb, gz, gy, gyb, gzb, ghome, gsave_y, gsave_z, gmid, glocal, slocal,
+    w_v, hbuf, base, pb, gz, gy, gyb, gzb, ghome, gsave_y, gsave_z, qmid, glocal, slocal,
     szb, ssend, syb, qsend, qb, s5b, s7b, zsend, gsend_t, gsend_z, gb,
     rs_s2, rs_r2, rs_s1, rs_s3, rs_r1, rs_r3, q_s2, q_r2, q_s1, q_s3, q_r1, q_r3,
-    gp, gp_z, gp_y, gpb, sums_a, sums_b, slab_a, slab_b, gout, mats_loc, mats_z, mats_y,
+    gp, gp_z, gp_y, gp_mid, gpf, gpb, sums_a, sums_b, slab_a, slab_b, gout, mats_loc, mats_z, mats_y,
     send_sem, recv_sem, w_sem,
 ):
     tokens = hid.shape[0]
     me = lax.axis_index("tensor")
     my_dp = lax.axis_index("dp")
     y, z = me // SIDE, lax.rem(me, SIDE)
-    z_of = lax.rem(y + z, SIDE)
     counter = [0]
 
     def mark(name):
@@ -218,11 +217,64 @@
         )
     pl.semaphore_wait(barrier, 15 + n_dp - 1)
 
-    cot_in, genz_in, geny_in = [], [], []
-    for d in range(1, 4):
-        cols = chunk_at(lax.rem(y + d + z, SIDE))
-        cot_in.append(send(cot.at[:, cols], gyb.at[y], at(d, 0)))
-        geny_in.append(send(gen.at[pl.ds(6, 2), :, cols], gy.at[y], at(d, 0)))
+    def cross(src_of, dst, own_slot, dev_of, always_remote):
+        index = ids(4)
+        sent = []
+        for d in range(4):
+            c = copy(
+                src_of(d), dst.at[own_slot], index + d, index + own_slot, {"tensor": dev_of(d)}
+            )
+            if d == 0:
+                keep = pltpu.make_async_copy(
+                    src_of(0), dst.at[own_slot], recv_sem.at[index + own_slot]
+                )
+                pl.when(always_remote)(lambda c=c: c.start())
+                pl.when(jnp.logical_not(always_remote))(lambda keep=keep: keep.start())
+            else:
+                c.start()
+            sent.append(c)
+        done = []
+
+        def arrive():
+            if not done:
+                done.append(True)
+                for m in range(4):
+                    pltpu.make_async_copy(dst.at[m], dst.at[m], recv_sem.at[index + m]).wait()
+
+        def finish():
+            arrive()
+            pl.when(always_remote)(lambda: sent[0].wait_send())
+            for c in sent[1:]:
+                c.wait_send()
+
+        endings.append(finish)
+        return arrive
+
+    def along_y(src, dst):
+        copies = [send(src.at[wrap(y + d, SIDE)], dst.at[y], at(d, 0)) for d in range(1, 4)]
+        dst[y] = src[y]
+        return copies
+
+    def along_z(src, dst, first=0):
+        copies = [
+            send(src.at[wrap(z + d, SIDE)], dst.at[first + z], at(0, d)) for d in range(1, 4)
+        ]
+        dst[first + z] = src[z]
+        return copies
+
+    def arrive_all(copies):
+        for c in copies:
+            c.arrive()
+
+    def turned(d):
+        return z * SIDE + wrap(z + d, SIDE)
+
+    cot_arrive = cross(
+        lambda d: cot.at[:, chunk_at(wrap(z + d, SIDE))], gyb, y, turned, y != z
+    )
+    geny_arrive = cross(
+        lambda d: gen.at[pl.ds(6, 2), :, chunk_at(wrap(z + d, SIDE))], gy, y, turned, y != z
+    )
 
     def held(dy, dz, lo, hi):
         ref = hid if (dy, dz) == (0, 0) else hbuf.at[dy, dz]
@@ -256,6 +308,7 @@
         routes.append(("y", "z", cut, tokens))
     first = [ring_start(a, 0, lo, hi) for a, _, lo, hi in routes]
     second = [{0: ring_start(b, 0, lo, hi)} for _, b, lo, hi in routes]
+    genz_in = []
     for d in range(1, 4):
         cols = chunk_at(wrap(z + d, SIDE))
         genz_in.append(send(gen.at[pl.ds(4, 2), :, cols], gz.at[z], at(0, d)))
@@ -286,8 +339,6 @@
                 c.arrive()
             base[...] += dot(hbuf[dy, dz], w_rows(-dy, -dz))
 
-    gyb[y] = cot[:, chunk_at(z_of)]
-    gy[y] = gen[6:8, :, chunk_at(z_of)]
     gz[z] = gen[4:6, :, chunk_at(z)]
 
     for k in range(3):
@@ -321,89 +372,37 @@
             for m in range(4):
                 target[m] = values[m].astype(BF16)
 
-    def cross(src, dst, own_slot, dev_of, src_of):
-        index = ids(4)
-        sent = []
-        for d in range(4):
-            c = copy(
-                src.at[src_of(d)], dst.at[own_slot], index + d, index + own_slot,
-                {"tensor": dev_of(d)},
-            )
-            if d == 0:
-                keep = pltpu.make_async_copy(
-                    src.at[src_of(0)], dst.at[own_slot], recv_sem.at[index + own_slot]
-                )
-                pl.when(dev_of(0) != me)(lambda c=c: c.start())
-                pl.when(dev_of(0) == me)(lambda keep=keep: keep.start())
-            else:
-                c.start()
-            sent.append(c)
-        done = []
-
-        def arrive():
-            if not done:
-                done.append(True)
-                for m in range(4):
-                    pltpu.make_async_copy(src.at[m], dst.at[m], recv_sem.at[index + m]).wait()
-
-        def finish():
-            arrive()
-            pl.when(dev_of(0) != me)(lambda: sent[0].wait_send())
-            for c in sent[1:]:
-                c.wait_send()
-
-        endings.append(finish)
-        return arrive
-
-    for c in geny_in:
-        c.arrive()
+    geny_arrive()
     fill_pairs(mats_y, gy)
-    for c in cot_in:
-        c.arrive()
+    cot_arrive()
     pairs_apply(dot_nt, (1, 0), gyb, mats_y, gsave_y, gsend_t)
-    step_in = []
-    for d in range(1, 4):
-        step_in.append(send(gsend_t.at[wrap(y + d, SIDE)], gmid.at[z_of], at(d, 0)))
-    gmid[z_of] = gsend_t[y]
+    step_in = along_y(gsend_t, gzb)
     mark("bwd_y")
 
     gather_second(0)
-    for c in genz_in:
-        c.arrive()
+    arrive_all(genz_in)
     fill_pairs(mats_z, gz)
-    for c in step_in:
-        c.arrive()
-    step_in = []
-    for d in range(1, 4):
-        step_in.append(send(gmid.at[wrap(z + d, SIDE)], gzb.at[z], at(0, d)))
-    gzb[z] = gmid[z]
     w_copy.wait()
     base[...] = dot(hid[...], w_rows(0, 0))
     mark("ag0")
 
     gather_first()
+    mark("ag1")
+    arrive_all(step_in)
+    pairs_apply(dot_nt, (1, 0), gzb, mats_z, gsave_z, gsend_z)
+    back_in = along_z(gsend_z, ghome)
+    mark("bwd_z")
     accumulate((1, 0), (3, 0), (0, 1), (0, 3))
-    mark("ag1")
+
     gather_far()
     accumulate((2, 0), (0, 2))
-
-    for c in step_in:
-        c.arrive()
-    pairs_apply(dot_nt, (1, 0), gzb, mats_z, gsave_z, gsend_z)
-    back_in = []
-    for d in range(1, 4):
-        back_in.append(send(gsend_z.at[wrap(z + d, SIDE)], ghome.at[z], at(0, d)))
-    ghome[z] = gsend_z[z]
-    mark("bwd_z")
-
     gather_second(1)
     accumulate((1, 1), (3, 1))
     gather_second(3)
     accumulate((1, 3), (3, 3))
     mark("ag2")
 
-    for c in back_in:
-        c.arrive()
+    arrive_all(back_in)
     ga = pair_of(ghome, 0, 1)
     gc = pair_of(ghome, 2, 3)
     glocal[3, 0], glocal[3, 1] = ga, gc
@@ -516,20 +515,20 @@
     for c in range(4):
         side = fc if c < 2 else fd
         ssend[c] = side[:, (c % 2) * LANES : (c % 2) * LANES + LANES].astype(BF16)
-    fwd_in = []
-    for d in range(1, 4):
-        fwd_in.append(send(ssend.at[wrap(z + d, SIDE)], szb.at[z], at(0, d)))
-    szb[z] = ssend[z]
+    fwd_in = along_z(ssend, szb)
     mark("fwd_local")
 
-    for fixed in (2, 1):
-        for s in sums:
-            s.near(fixed)
+    def near(*blocks):
+        for fixed in blocks:
+            for s in sums:
+                s.near(fixed)
+
+    near(2)
     mark("near1")
 
     def put_local(k, s, value):
         for j in range(2):
-            gp[pl.ds(((k // 2) * 4 + 2 * s + j) * 128 + (k % 2) * 64, 64)] = value[
+            gp[(k // 2) * 4 + 2 * s + j, (k % 2) * 64 : (k % 2) * 64 + 64] = value[
                 :, j * LANES : (j + 1) * LANES
             ]
 
@@ -544,21 +543,10 @@
             ),
         )
 
-    for c in fwd_in:
-        c.arrive()
+    arrive_all(fwd_in)
     pairs_apply(dot, (0, 1), szb, mats_z, s5b, zsend)
-    fwd_arrive = cross(
-        zsend, syb, y,
-        lambda d: ((SIDE - d) % SIDE) * SIDE + wrap(z + d, SIDE),
-        lambda d: wrap(z + d, SIDE),
-    )
+    fwd_in = along_y(zsend, syb)
     mark("fwd_z")
-    for fixed in (3, 0):
-        for s in sums:
-            s.near(fixed)
-    for s in sums:
-        s.last_far()
-    mark("near2")
 
     def pair_grads(states, grads, dst):
         for k in range(2):
@@ -567,30 +555,19 @@
                 dst[a, k * 64 : k * 64 + 64] = value[:, :LANES]
                 dst[b, k * 64 : k * 64 + 64] = value[:, LANES:]
 
-    def piece(index):
-        return pl.ds(pl.multiple_of(index * 128, 128), 128)
-
     pair_grads((szb, s5b), (gsave_z, gzb), gp_z)
-    outz_in = []
-    for d in range(1, 4):
-        outz_in.append(send(gp_z.at[wrap(z + d, SIDE)], gp.at[piece(8 + z)], at(0, d)))
-    gp[piece(8 + z)] = gp_z[z]
-
-    fwd_arrive()
+    outz_in = along_z(gp_z, gp, 8)
+    near(1)
+
+    arrive_all(fwd_in)
     pairs_apply(dot, (0, 1), syb, mats_y, s7b, qsend)
-    query_in = []
-    for d in range(1, 4):
-        query_in.append(send(qsend.at[wrap(y + d, SIDE)], qb.at[z_of], at(d, 0)))
-    qb[z_of] = qsend[y]
+    query_in = along_y(qsend, qmid)
     mark("fwd_y")
-
     pair_grads((syb, s7b), (gsave_y, gyb), gp_y)
-    outy_in = []
-    for d in range(1, 4):
-        outy_in.append(send(gp_y.at[wrap(y + d, SIDE)], gp.at[piece(12 + z_of)], at(d, 0)))
-    gp[piece(12 + z_of)] = gp_y[y]
+    outy_in = along_y(gp_y, gp_mid)
     mark("grads")
 
+    near(3)
     class Slabs:
         def __init__(self, start, size, sums_ref, slab_ref):
             self.start, self.size = start, size
@@ -601,14 +578,16 @@
             return pl.ds(pl.multiple_of(self.start + dev * self.size, 32), self.size)
 
         def scatter(self):
-            all_rows = pl.ds(self.start, 16 * self.size)
-            gpb[all_rows] = gp[all_rows].astype(BF16)
+            first, count = self.start // 128, 16 * self.size // 128
+            for i in range(first, first + count):
+                gpf[pl.ds(i * 128, 128)] = gp[i]
+                gpb[pl.ds(i * 128, 128)] = gp[i].astype(BF16)
             for d in range(1, n_dp):
                 dev = lax.rem(my_dp + d, n_dp)
                 self.ins.append(send(gpb.at[self.rows(dev)], self.sums_ref.at[d], dev, "dp"))
 
         def gather(self):
-            total = gp[self.rows(my_dp)]
+            total = gpf[self.rows(my_dp)]
             for d, c in zip(range(1, n_dp), self.ins):
                 c.arrive()
                 total = total + self.sums_ref[d].astype(F32)
@@ -622,26 +601,30 @@
             for c in self.outs:
                 c.arrive()
 
+    early, late = Slabs(0, 96, sums_a, slab_a), Slabs(1536, 32, sums_b, slab_b)
+    arrive_all(outy_in)
+    outy_in = along_z(gp_mid, gp, 12)
+    arrive_all(query_in)
+    query_in = along_z(qmid, qb)
+    arrive_all(outz_in)
+    if n_dp > 1:
+        early.scatter()
+    near(0)
+    for s in sums:
+        s.last_far()
+    mark("near2")
+    arrive_all(outy_in)
+    if n_dp > 1:
+        late.scatter()
+        early.gather()
     for s in sums:
         s.last_near()
     mark("last_near")
-    early, late = Slabs(0, 96, sums_a, slab_a), Slabs(1536, 32, sums_b, slab_b)
-    for c in outz_in:
-        c.arrive()
-    if n_dp > 1:
-        early.scatter()
-
-    for c in outy_in:
-        c.arrive()
-    if n_dp > 1:
-        late.scatter()
-        early.gather()
     if n_dp > 1:
         late.gather()
     mark("dp")
 
-    for c in query_in:
-        c.arrive()
+    arrive_all(query_in)
     for c in range(4):
         query[:, c * LANES : (c + 1) * LANES] = qb[c]
     mark("query")
@@ -651,13 +634,12 @@
     if n_dp > 1:
         early.finish()
         late.finish()
-    final = gout if n_dp > 1 else gp
     for pair in range(4):
         for c in range(4):
+            i = pair * 4 + c
+            value = gout[pl.ds(i * 128, 128)] if n_dp > 1 else gp[i]
             for j in range(2):
-                ggrad[2 * pair + j, :, c * LANES : (c + 1) * LANES] = final[
-                    pl.ds((pair * 4 + c) * 128 + j * 64, 64)
-                ]
+                ggrad[2 * pair + j, :, c * LANES : (c + 1) * LANES] = value[j * 64 : j * 64 + 64]
 
 
 def main_call(hidden, weight, generators, cotangent, n_dp=1, scale=1.0):
@@ -696,9 +678,11 @@
             block,
             blocks, blocks, blocks, blocks, blocks, blocks,
             block, block, block, block, block, block,
-            vm(2048, 128, dtype=F32),
+            vm(16, 128, 128, dtype=F32),
             vm(4, 128, 128, dtype=F32),
             vm(4, 128, 128, dtype=F32),
+            vm(4, 128, 128, dtype=F32),
+            vm(2048, 128, dtype=F32),
             vm(2048, 128),
             vm(16, 96, 128),
             vm(16, 32, 128),

time: 170 us -> 197 us (1.16)
  Pallas kernels: 169 us -> 196 us
    pallas_call x1, Pallas kernels: 166 us -> 193 us  [main_call(): pl.pallas_call(functools.partial(main_kernel, n_dp, scale), out_shape=(ja...]
where the time goes in v4:
time: 197 us; the launch traced here: 196 us
  Pallas kernels  196 us (99%)
    pallas_call x1, Pallas kernels, main_call(): pl.pallas_call(functools.partial(main_kernel, n_dp, scale), out_shape=(ja...  193 us

profile of v4, /device:TPU:1, one launch (start us, length us, event | category | flops | bytes accessed | tf_op | source)
XLA Modules:
  0.0 196.5 jit_solution(4007261766265328986)
XLA Ops:
  0.6 193.1 %adapt.1 = (bf16[384,512]{1,0:T(8,128)(2,1)}, bf16[384,512]{1,0:T(8,128)(2,1)}, f32[8,64,512]{2,1,0:T(8,128)}) custom-call(bf16[384,512]{1,0:T(8,128)(2,1)} %refs_0_.1, bf16[8192,512]{1,0:T(8,128)(2,1)} %refs_1_.1, f32[8,64,512]{2,1,0:T(8,128)} %refs_2_.1, bf16[384,512]{1,0:T(8,128)(2,1)} %refs_3_.1), custom_call_target="tpu_custom_call" | custom-call | flops 6442450944 | bytes 12582912 | tf_op jit(solution)/shard_map/adapt/pallas_call | solution.py:652
  193.8 2.7 %results.1 = (bf16[384,512]{1,0:T(8,128)(2,1)}, bf16[384,512]{1,0:T(8,128)(2,1)}, f32[8,64,512]{2,1,0:T(8,128)}) custom-call(bf16[384,512]{1,0:T(8,128)(2,1)} %get-tuple-element.6.refs_0_, bf16[384,512]{1,0:T(8,128)(2,1)} %get-tuple-element.7.refs_1_, f32[8,64,512]{2,1,0:T(8,128)} %get-tuple-element.8.refs_2_), custom_call_target="tpu_custom_call" | custom-call | tf_op jit(solution)/shard_map/results/pallas_call | solution.py:717

commit v5 on v3

--- a/solution.py
+++ b/solution.py
@@ -111,10 +111,15 @@
 
 
 PAIRS = (((0, 1), (2, 3)), ((0, 2), (1, 3)))
-N_SEMS = 224
-SPLIT_GATHER = 320
-SPLIT_SUM = 320
+N_SEMS = 320
+GATHER = (("z", "y", 0, 160), ("z", "y", 160, 320), ("y", "z", 320, 384))
+SUM = (("y", "z", 0, 160), ("y", "z", 160, 320), ("z", "y", 320, 384))
 STOP = None
+
+
+def parts_of(table, tokens):
+    scaled = [(a, b, lo * tokens // 384 // 32 * 32, hi * tokens // 384 // 32 * 32) for a, b, lo, hi in table]
+    return [part for part in scaled if part[2] < part[3]]
 
 
 class Stop(Exception):
@@ -147,7 +152,7 @@
 def main_body(
     n_dp, scale, pending, endings,
     hid, wt, gen, cot, query, igrad, ggrad,
-    w_v, hbuf, base, pb, gz, gy, gyb, gzb, ghome, gsave_y, gsave_z, gmid, glocal, slocal,
+    w_v, hbuf, base, pb, gz, gy, gyb, gzb, ghome, gsave_y, gsave_z, gmid, cotc, genc, glocal, slocal,
     szb, ssend, syb, qsend, qb, s5b, s7b, zsend, gsend_t, gsend_z, gb,
     rs_s2, rs_r2, rs_s1, rs_s3, rs_r1, rs_r3, q_s2, q_r2, q_s1, q_s3, q_r1, q_r3,
     gp, gp_z, gp_y, gpb, sums_a, sums_b, slab_a, slab_b, gout, mats_loc, mats_z, mats_y,
@@ -201,11 +206,11 @@
     def w_rows(dy, dz):
         return w_v[pl.ds(pl.multiple_of(at(dy, dz) * 512, 512), 512), :]
 
-    def chunk_at(index):
-        return pl.ds(pl.multiple_of(index * LANES, LANES), LANES)
-
     w_copy = pltpu.make_async_copy(wt, w_v, w_sem)
-    w_copy.start()
+    for c in range(4):
+        cols = slice(c * LANES, (c + 1) * LANES)
+        cotc[c] = cot[:, cols]
+        genc[c] = gen[4:8, :, cols]
 
     barrier = pltpu.get_barrier_semaphore()
     for d in range(1, 16):
@@ -220,9 +225,9 @@
 
     cot_in, genz_in, geny_in = [], [], []
     for d in range(1, 4):
-        cols = chunk_at(lax.rem(y + d + z, SIDE))
-        cot_in.append(send(cot.at[:, cols], gyb.at[y], at(d, 0)))
-        geny_in.append(send(gen.at[pl.ds(6, 2), :, cols], gy.at[y], at(d, 0)))
+        c = lax.rem(y + d + z, SIDE)
+        cot_in.append(send(cotc.at[c], gyb.at[y], at(d, 0)))
+        geny_in.append(send(genc.at[c, pl.ds(2, 2)], gy.at[y], at(d, 0)))
 
     def held(dy, dz, lo, hi):
         ref = hid if (dy, dz) == (0, 0) else hbuf.at[dy, dz]
@@ -250,15 +255,13 @@
         copies[1].arrive()
         copies.append(hop(axis, fixed, 3, -1, middle, hi))
 
-    cut = SPLIT_GATHER * tokens // 384 // 32 * 32
-    routes = [("z", "y", 0, cut)]
-    if cut < tokens:
-        routes.append(("y", "z", cut, tokens))
+    routes = parts_of(GATHER, tokens)
     first = [ring_start(a, 0, lo, hi) for a, _, lo, hi in routes]
     second = [{0: ring_start(b, 0, lo, hi)} for _, b, lo, hi in routes]
     for d in range(1, 4):
-        cols = chunk_at(wrap(z + d, SIDE))
-        genz_in.append(send(gen.at[pl.ds(4, 2), :, cols], gz.at[z], at(0, d)))
+        genz_in.append(send(genc.at[wrap(z + d, SIDE), pl.ds(0, 2)], gz.at[z], at(0, d)))
+
+    w_copy.start()
 
     def gather_second(step):
         for (_, b, lo, hi), copies in zip(routes, second):
@@ -286,9 +289,9 @@
                 c.arrive()
             base[...] += dot(hbuf[dy, dz], w_rows(-dy, -dz))
 
-    gyb[y] = cot[:, chunk_at(z_of)]
-    gy[y] = gen[6:8, :, chunk_at(z_of)]
-    gz[z] = gen[4:6, :, chunk_at(z)]
+    gyb[y] = cotc[z_of]
+    gy[y] = genc[z_of, 2:4]
+    gz[z] = genc[z, 0:2]
 
     for k in range(3):
         for s in range(2):
@@ -382,11 +385,7 @@
     mark("ag0")
 
     gather_first()
-    accumulate((1, 0), (3, 0), (0, 1), (0, 3))
     mark("ag1")
-    gather_far()
-    accumulate((2, 0), (0, 2))
-
     for c in step_in:
         c.arrive()
     pairs_apply(dot_nt, (1, 0), gzb, mats_z, gsave_z, gsend_z)
@@ -396,10 +395,11 @@
     ghome[z] = gsend_z[z]
     mark("bwd_z")
 
+    gather_far()
+    accumulate((1, 0), (3, 0), (0, 1), (0, 3))
     gather_second(1)
-    accumulate((1, 1), (3, 1))
     gather_second(3)
-    accumulate((1, 3), (3, 3))
+    accumulate((2, 0), (0, 2), (1, 1), (3, 1))
     mark("ag2")
 
     for c in back_in:
@@ -418,7 +418,6 @@
     mark("bwd_local")
 
     gather_second(2)
-    accumulate((1, 2), (3, 2))
     mark("ag3")
 
     computed = set()
@@ -494,14 +493,20 @@
             q = q + q_r1[self.rows].astype(F32) + q_r3[self.rows].astype(F32)
             igrad[self.rows] = q.astype(BF16)
 
-    cut = SPLIT_SUM * tokens // 384 // 32 * 32
-    sums = [Sum("y", "z", 0, cut)]
-    if cut < tokens:
-        sums.append(Sum("z", "y", cut, tokens))
-    for fixed in (2, 1, 3, 0):
-        for s in sums:
-            s.far(fixed)
+    sums = [Sum(*part) for part in parts_of(SUM, tokens)]
+    def far(group, *blocks):
+        for fixed in blocks:
+            for s in group:
+                s.far(fixed)
+
+    def near(group, *blocks):
+        for fixed in blocks:
+            for s in group:
+                s.near(fixed)
+
+    far(sums, 2, 1, 3, 0)
     mark("rs_far")
+    accumulate((1, 3), (3, 3), (1, 2), (3, 2))
 
     accumulate((2, 1), (2, 3), (2, 2))
     mark("base")
@@ -522,9 +527,7 @@
     szb[z] = ssend[z]
     mark("fwd_local")
 
-    for fixed in (2, 1):
-        for s in sums:
-            s.near(fixed)
+    near(sums, 2, 1)
     mark("near1")
 
     def put_local(k, s, value):
@@ -553,9 +556,7 @@
         lambda d: wrap(z + d, SIDE),
     )
     mark("fwd_z")
-    for fixed in (3, 0):
-        for s in sums:
-            s.near(fixed)
+    near(sums, 3, 0)
     for s in sums:
         s.last_far()
     mark("near2")
@@ -612,7 +613,7 @@
             for d, c in zip(range(1, n_dp), self.ins):
                 c.arrive()
                 total = total + self.sums_ref[d].astype(F32)
-            self.slab_ref[...] = total * scale
+            self.slab_ref[...] = (total * scale).astype(BF16)
             for d in range(1, n_dp):
                 dev = lax.rem(my_dp + d, n_dp)
                 self.outs.append(send(self.slab_ref, gout.at[self.rows(my_dp)], dev, "dp"))
@@ -622,21 +623,19 @@
             for c in self.outs:
                 c.arrive()
 
+    early, late = Slabs(0, 96, sums_a, slab_a), Slabs(1536, 32, sums_b, slab_b)
+    for c in outz_in:
+        c.arrive()
+    if n_dp > 1:
+        early.scatter()
     for s in sums:
         s.last_near()
     mark("last_near")
-    early, late = Slabs(0, 96, sums_a, slab_a), Slabs(1536, 32, sums_b, slab_b)
-    for c in outz_in:
-        c.arrive()
-    if n_dp > 1:
-        early.scatter()
-
     for c in outy_in:
         c.arrive()
     if n_dp > 1:
         late.scatter()
         early.gather()
-    if n_dp > 1:
         late.gather()
     mark("dp")
 
@@ -654,10 +653,9 @@
     final = gout if n_dp > 1 else gp
     for pair in range(4):
         for c in range(4):
+            value = final[pl.ds((pair * 4 + c) * 128, 128)].astype(F32)
             for j in range(2):
-                ggrad[2 * pair + j, :, c * LANES : (c + 1) * LANES] = final[
-                    pl.ds((pair * 4 + c) * 128 + j * 64, 64)
-                ]
+                ggrad[2 * pair + j, :, c * LANES : (c + 1) * LANES] = value[j * 64 : j * 64 + 64]
 
 
 def main_call(hidden, weight, generators, cotangent, n_dp=1, scale=1.0):
@@ -689,6 +687,7 @@
             vm(4, 2, 64, LANES, dtype=F32),
             vm(4, 2, 64, LANES, dtype=F32),
             chunks, chunks, chunks, chunks, chunks, chunks,
+            chunks, vm(4, 4, 64, LANES, dtype=F32),
             vm(4, 2, tokens, 256),
             vm(4, 2, tokens, 256),
             chunks, chunks, chunks, chunks, chunks,
@@ -702,9 +701,9 @@
             vm(2048, 128),
             vm(16, 96, 128),
             vm(16, 32, 128),
-            vm(96, 128, dtype=F32),
-            vm(32, 128, dtype=F32),
-            vm(2048, 128, dtype=F32),
+            vm(96, 128),
+            vm(32, 128),
+            vm(2048, 128),
             vm(5, 2, 2, 256, 256),
             vm(2, 2, 2, 256, 256),
             vm(2, 2, 2, 256, 256),

time: 170 us -> 164 us (0.965)
  Pallas kernels: 169 us -> 163 us
    pallas_call x1, Pallas kernels: 166 us -> 161 us  [main_call(): pl.pallas_call(functools.partial(main_kernel, n_dp, scale), out_shape=(ja...]
where the time goes in v5:
time: 164 us
  Pallas kernels  163 us (99%)
    pallas_call x1, Pallas kernels, main_call(): pl.pallas_call(functools.partial(main_kernel, n_dp, scale), out_shape=(ja...  161 us

profile of v5, /device:TPU:1, one launch (start us, length us, event | category | flops | bytes accessed | tf_op | source)
XLA Modules:
  0.0 164.1 jit_solution(17183154248693286970)
XLA Ops:
  0.6 160.7 %adapt.1 = (bf16[384,512]{1,0:T(8,128)(2,1)}, bf16[384,512]{1,0:T(8,128)(2,1)}, f32[8,64,512]{2,1,0:T(8,128)}) custom-call(bf16[384,512]{1,0:T(8,128)(2,1)} %refs_0_.1, bf16[8192,512]{1,0:T(8,128)(2,1)} %refs_1_.1, f32[8,64,512]{2,1,0:T(8,128)} %refs_2_.1, bf16[384,512]{1,0:T(8,128)(2,1)} %refs_3_.1), custom_call_target="tpu_custom_call" | custom-call | flops 6442450944 | bytes 12582912 | tf_op jit(solution)/shard_map/adapt/pallas_call | solution.py:668
  161.4 2.7 %results.1 = (bf16[384,512]{1,0:T(8,128)(2,1)}, bf16[384,512]{1,0:T(8,128)(2,1)}, f32[8,64,512]{2,1,0:T(8,128)}) custom-call(bf16[384,512]{1,0:T(8,128)(2,1)} %get-tuple-element.6.refs_0_, bf16[384,512]{1,0:T(8,128)(2,1)} %get-tuple-element.7.refs_1_, f32[8,64,512]{2,1,0:T(8,128)} %get-tuple-element.8.refs_2_), custom_call_target="tpu_custom_call" | custom-call | tf_op jit(solution)/shard_map/results/pallas_call | solution.py:732

commit v6 on v5

--- a/solution.py
+++ b/solution.py
@@ -112,8 +112,8 @@
 
 PAIRS = (((0, 1), (2, 3)), ((0, 2), (1, 3)))
 N_SEMS = 320
-GATHER = (("z", "y", 0, 160), ("z", "y", 160, 320), ("y", "z", 320, 384))
-SUM = (("y", "z", 0, 160), ("y", "z", 160, 320), ("z", "y", 320, 384))
+GATHER = (("z", "y", 0, 160), ("z", "y", 160, 352), ("y", "z", 352, 384))
+SUM = (("y", "z", 0, 160), ("y", "z", 160, 352), ("z", "y", 352, 384))
 STOP = None
 
 
@@ -263,13 +263,15 @@
 
     w_copy.start()
 
-    def gather_second(step):
-        for (_, b, lo, hi), copies in zip(routes, second):
-            ring_forward(b, step, lo, hi, copies[step])
-
-    def gather_first():
-        for (a, b, lo, hi), ring, copies in zip(routes, first, second):
-            middle = (lo + hi) // 2
+    def gather_second(step, parts):
+        for i in parts:
+            _, b, lo, hi = routes[i]
+            ring_forward(b, step, lo, hi, second[i][step])
+
+    def gather_first(parts):
+        for i in parts:
+            a, b, lo, hi = routes[i]
+            ring, copies, middle = first[i], second[i], (lo + hi) // 2
             ring[0].arrive()
             ring.append(hop(a, 0, 1, 1, lo, middle))
             copies[1] = ring_start(b, 1, lo, hi)
@@ -277,11 +279,15 @@
             ring.append(hop(a, 0, 3, -1, middle, hi))
             copies[3] = ring_start(b, 3, lo, hi)
 
-    def gather_far():
-        for (_, b, lo, hi), ring, copies in zip(routes, first, second):
-            ring[2].arrive()
-            ring[3].arrive()
-            copies[2] = ring_start(b, 2, lo, hi)
+    def gather_far(parts):
+        for i in parts:
+            _, b, lo, hi = routes[i]
+            first[i][2].arrive()
+            first[i][3].arrive()
+            second[i][2] = ring_start(b, 2, lo, hi)
+
+    z_parts = [i for i, part in enumerate(routes) if part[0] == "z"]
+    y_parts = [i for i, part in enumerate(routes) if part[0] == "y"]
 
     def accumulate(*blocks):
         for dy, dz in blocks:
@@ -370,7 +376,7 @@
     gmid[z_of] = gsend_t[y]
     mark("bwd_y")
 
-    gather_second(0)
+    gather_second(0, z_parts)
     for c in genz_in:
         c.arrive()
     fill_pairs(mats_z, gz)
@@ -380,11 +386,13 @@
     for d in range(1, 4):
         step_in.append(send(gmid.at[wrap(z + d, SIDE)], gzb.at[z], at(0, d)))
     gzb[z] = gmid[z]
+    mark("ag0")
+
+    gather_first(z_parts)
+    gather_first(y_parts)
+    gather_second(0, y_parts)
     w_copy.wait()
     base[...] = dot(hid[...], w_rows(0, 0))
-    mark("ag0")
-
-    gather_first()
     mark("ag1")
     for c in step_in:
         c.arrive()
@@ -395,11 +403,11 @@
     ghome[z] = gsend_z[z]
     mark("bwd_z")
 
-    gather_far()
+    gather_far(z_parts)
+    gather_second(1, z_parts)
+    gather_second(3, z_parts)
+    gather_far(y_parts)
     accumulate((1, 0), (3, 0), (0, 1), (0, 3))
-    gather_second(1)
-    gather_second(3)
-    accumulate((2, 0), (0, 2), (1, 1), (3, 1))
     mark("ag2")
 
     for c in back_in:
@@ -417,7 +425,10 @@
     gb[:, 256:] = fb.astype(BF16)
     mark("bwd_local")
 
-    gather_second(2)
+    gather_second(1, y_parts)
+    gather_second(3, y_parts)
+    gather_second(2, z_parts)
+    gather_second(2, y_parts)
     mark("ag3")
 
     computed = set()
@@ -506,7 +517,7 @@
 
     far(sums, 2, 1, 3, 0)
     mark("rs_far")
-    accumulate((1, 3), (3, 3), (1, 2), (3, 2))
+    accumulate((2, 0), (0, 2), (1, 1), (3, 1), (1, 3), (3, 3), (1, 2), (3, 2))
 
     accumulate((2, 1), (2, 3), (2, 2))
     mark("base")
@@ -547,51 +558,6 @@
             ),
         )
 
-    for c in fwd_in:
-        c.arrive()
-    pairs_apply(dot, (0, 1), szb, mats_z, s5b, zsend)
-    fwd_arrive = cross(
-        zsend, syb, y,
-        lambda d: ((SIDE - d) % SIDE) * SIDE + wrap(z + d, SIDE),
-        lambda d: wrap(z + d, SIDE),
-    )
-    mark("fwd_z")
-    near(sums, 3, 0)
-    for s in sums:
-        s.last_far()
-    mark("near2")
-
-    def pair_grads(states, grads, dst):
-        for k in range(2):
-            for i, (a, b) in enumerate(PAIRS[k]):
-                value = pair_extract(dot_tn(pair_of(states[k], a, b), pair_of(grads[k], a, b)))
-                dst[a, k * 64 : k * 64 + 64] = value[:, :LANES]
-                dst[b, k * 64 : k * 64 + 64] = value[:, LANES:]
-
-    def piece(index):
-        return pl.ds(pl.multiple_of(index * 128, 128), 128)
-
-    pair_grads((szb, s5b), (gsave_z, gzb), gp_z)
-    outz_in = []
-    for d in range(1, 4):
-        outz_in.append(send(gp_z.at[wrap(z + d, SIDE)], gp.at[piece(8 + z)], at(0, d)))
-    gp[piece(8 + z)] = gp_z[z]
-
-    fwd_arrive()
-    pairs_apply(dot, (0, 1), syb, mats_y, s7b, qsend)
-    query_in = []
-    for d in range(1, 4):
-        query_in.append(send(qsend.at[wrap(y + d, SIDE)], qb.at[z_of], at(d, 0)))
-    qb[z_of] = qsend[y]
-    mark("fwd_y")
-
-    pair_grads((syb, s7b), (gsave_y, gyb), gp_y)
-    outy_in = []
-    for d in range(1, 4):
-        outy_in.append(send(gp_y.at[wrap(y + d, SIDE)], gp.at[piece(12 + z_of)], at(d, 0)))
-    gp[piece(12 + z_of)] = gp_y[y]
-    mark("grads")
-
     class Slabs:
         def __init__(self, start, size, sums_ref, slab_ref):
             self.start, self.size = start, size
@@ -623,19 +589,74 @@
             for c in self.outs:
                 c.arrive()
 
-    early, late = Slabs(0, 96, sums_a, slab_a), Slabs(1536, 32, sums_b, slab_b)
-    for c in outz_in:
-        c.arrive()
+    early, late = Slabs(0, 64, sums_a, slab_a), Slabs(1024, 64, sums_b, slab_b)
+
+    for c in fwd_in:
+        c.arrive()
+    pairs_apply(dot, (0, 1), szb, mats_z, s5b, zsend)
+    fwd_arrive = cross(
+        zsend, syb, y,
+        lambda d: ((SIDE - d) % SIDE) * SIDE + wrap(z + d, SIDE),
+        lambda d: wrap(z + d, SIDE),
+    )
     if n_dp > 1:
         early.scatter()
+    mark("fwd_z")
+    near(sums, 3)
     for s in sums:
-        s.last_near()
+        if s.a == "y":
+            s.last_far()
+    mark("near2")
+
+    def pair_grads(states, grads, dst):
+        for k in range(2):
+            for i, (a, b) in enumerate(PAIRS[k]):
+                value = pair_extract(dot_tn(pair_of(states[k], a, b), pair_of(grads[k], a, b)))
+                dst[a, k * 64 : k * 64 + 64] = value[:, :LANES]
+                dst[b, k * 64 : k * 64 + 64] = value[:, LANES:]
+
+    def piece(index):
+        return pl.ds(pl.multiple_of(index * 128, 128), 128)
+
+    pair_grads((szb, s5b), (gsave_z, gzb), gp_z)
+    outz_in = []
+    for d in range(1, 4):
+        outz_in.append(send(gp_z.at[wrap(z + d, SIDE)], gp.at[piece(8 + z)], at(0, d)))
+    gp[piece(8 + z)] = gp_z[z]
+
+    fwd_arrive()
+    pairs_apply(dot, (0, 1), syb, mats_y, s7b, qsend)
+    query_in = []
+    for d in range(1, 4):
+        query_in.append(send(qsend.at[wrap(y + d, SIDE)], qb.at[z_of], at(d, 0)))
+    qb[z_of] = qsend[y]
+    mark("fwd_y")
+
+    pair_grads((syb, s7b), (gsave_y, gyb), gp_y)
+    outy_in = []
+    for d in range(1, 4):
+        outy_in.append(send(gp_y.at[wrap(y + d, SIDE)], gp.at[piece(12 + z_of)], at(d, 0)))
+    gp[piece(12 + z_of)] = gp_y[y]
+    mark("grads")
+
+    near(sums, 0)
+    for s in sums:
+        if s.a == "z":
+            s.last_far()
+    for s in sums:
+        if s.a == "y":
+            s.last_near()
     mark("last_near")
-    for c in outy_in:
+    if n_dp > 1:
+        early.gather()
+    for c in outz_in + outy_in:
         c.arrive()
     if n_dp > 1:
         late.scatter()
-        early.gather()
+    for s in sums:
+        if s.a == "z":
+            s.last_near()
+    if n_dp > 1:
         late.gather()
     mark("dp")
 
@@ -699,10 +720,10 @@
             vm(4, 128, 128, dtype=F32),
             vm(4, 128, 128, dtype=F32),
             vm(2048, 128),
-            vm(16, 96, 128),
-            vm(16, 32, 128),
-            vm(96, 128),
-            vm(32, 128),
+            vm(16, 64, 128),
+            vm(16, 64, 128),
+            vm(64, 128),
+            vm(64, 128),
             vm(2048, 128),
             vm(5, 2, 2, 256, 256),
             vm(2, 2, 2, 256, 256),

time: 164 us -> 159 us (0.970)
  Pallas kernels: 163 us -> 158 us
    pallas_call x1, Pallas kernels: 161 us -> 156 us  [main_call(): pl.pallas_call(functools.partial(main_kernel, n_dp, scale), out_shape=(ja...]
where the time goes in v6:
time: 159 us
  Pallas kernels  158 us (99%)
    pallas_call x1, Pallas kernels, main_call(): pl.pallas_call(functools.partial(main_kernel, n_dp, scale), out_shape=(ja...  156 us

profile of v6, /device:TPU:1, one launch (start us, length us, event | category | flops | bytes accessed | tf_op | source)
XLA Modules:
  0.0 159.0 jit_solution(121993024074821126)
XLA Ops:
  0.6 155.6 %adapt.1 = (bf16[384,512]{1,0:T(8,128)(2,1)}, bf16[384,512]{1,0:T(8,128)(2,1)}, f32[8,64,512]{2,1,0:T(8,128)}) custom-call(bf16[384,512]{1,0:T(8,128)(2,1)} %refs_0_.1, bf16[8192,512]{1,0:T(8,128)(2,1)} %refs_1_.1, f32[8,64,512]{2,1,0:T(8,128)} %refs_2_.1, bf16[384,512]{1,0:T(8,128)(2,1)} %refs_3_.1), custom_call_target="tpu_custom_call" | custom-call | flops 6442450944 | bytes 12582912 | tf_op jit(solution)/shard_map/adapt/pallas_call | solution.py:689
  156.3 2.7 %results.1 = (bf16[384,512]{1,0:T(8,128)(2,1)}, bf16[384,512]{1,0:T(8,128)(2,1)}, f32[8,64,512]{2,1,0:T(8,128)}) custom-call(bf16[384,512]{1,0:T(8,128)(2,1)} %get-tuple-element.6.refs_0_, bf16[384,512]{1,0:T(8,128)(2,1)} %get-tuple-element.7.refs_1_, f32[8,64,512]{2,1,0:T(8,128)} %get-tuple-element.8.refs_2_), custom_call_target="tpu_custom_call" | custom-call | tf_op jit(solution)/shard_map/results/pallas_call | solution.py:753

commit v7 on v5

--- a/solution.py
+++ b/solution.py
@@ -112,8 +112,8 @@
 
 PAIRS = (((0, 1), (2, 3)), ((0, 2), (1, 3)))
 N_SEMS = 320
-GATHER = (("z", "y", 0, 160), ("z", "y", 160, 320), ("y", "z", 320, 384))
-SUM = (("y", "z", 0, 160), ("y", "z", 160, 320), ("z", "y", 320, 384))
+GATHER = (("z", "y", 0, 160), ("z", "y", 160, 352), ("y", "z", 352, 384))
+SUM = (("y", "z", 0, 160), ("y", "z", 160, 352), ("z", "y", 352, 384))
 STOP = None
 
 

time: 164 us -> 157 us (0.957)
  Pallas kernels: 163 us -> 156 us
    pallas_call x1, Pallas kernels: 161 us -> 153 us  [main_call(): pl.pallas_call(functools.partial(main_kernel, n_dp, scale), out_shape=(ja...]
where the time goes in v7:
time: 157 us
  Pallas kernels  156 us (99%)
    pallas_call x1, Pallas kernels, main_call(): pl.pallas_call(functools.partial(main_kernel, n_dp, scale), out_shape=(ja...  153 us

profile of v7, /device:TPU:1, one launch (start us, length us, event | category | flops | bytes accessed | tf_op | source)
XLA Modules:
  0.0 156.8 jit_solution(10067129660188722738)
XLA Ops:
  0.6 153.4 %adapt.1 = (bf16[384,512]{1,0:T(8,128)(2,1)}, bf16[384,512]{1,0:T(8,128)(2,1)}, f32[8,64,512]{2,1,0:T(8,128)}) custom-call(bf16[384,512]{1,0:T(8,128)(2,1)} %refs_0_.1, bf16[8192,512]{1,0:T(8,128)(2,1)} %refs_1_.1, f32[8,64,512]{2,1,0:T(8,128)} %refs_2_.1, bf16[384,512]{1,0:T(8,128)(2,1)} %refs_3_.1), custom_call_target="tpu_custom_call" | custom-call | flops 6442450944 | bytes 12582912 | tf_op jit(solution)/shard_map/adapt/pallas_call | solution.py:668
  154.1 2.7 %results.1 = (bf16[384,512]{1,0:T(8,128)(2,1)}, bf16[384,512]{1,0:T(8,128)(2,1)}, f32[8,64,512]{2,1,0:T(8,128)}) custom-call(bf16[384,512]{1,0:T(8,128)(2,1)} %get-tuple-element.6.refs_0_, bf16[384,512]{1,0:T(8,128)(2,1)} %get-tuple-element.7.refs_1_, f32[8,64,512]{2,1,0:T(8,128)} %get-tuple-element.8.refs_2_), custom_call_target="tpu_custom_call" | custom-call | tf_op jit(solution)/shard_map/results/pallas_call | solution.py:732

commit v8 on v7

--- a/solution.py
+++ b/solution.py
@@ -263,13 +263,15 @@
 
     w_copy.start()
 
-    def gather_second(step):
-        for (_, b, lo, hi), copies in zip(routes, second):
-            ring_forward(b, step, lo, hi, copies[step])
-
-    def gather_first():
-        for (a, b, lo, hi), ring, copies in zip(routes, first, second):
-            middle = (lo + hi) // 2
+    def gather_second(step, parts):
+        for i in parts:
+            _, b, lo, hi = routes[i]
+            ring_forward(b, step, lo, hi, second[i][step])
+
+    def gather_first(parts):
+        for i in parts:
+            a, b, lo, hi = routes[i]
+            ring, copies, middle = first[i], second[i], (lo + hi) // 2
             ring[0].arrive()
             ring.append(hop(a, 0, 1, 1, lo, middle))
             copies[1] = ring_start(b, 1, lo, hi)
@@ -277,11 +279,15 @@
             ring.append(hop(a, 0, 3, -1, middle, hi))
             copies[3] = ring_start(b, 3, lo, hi)
 
-    def gather_far():
-        for (_, b, lo, hi), ring, copies in zip(routes, first, second):
-            ring[2].arrive()
-            ring[3].arrive()
-            copies[2] = ring_start(b, 2, lo, hi)
+    def gather_far(parts):
+        for i in parts:
+            _, b, lo, hi = routes[i]
+            first[i][2].arrive()
+            first[i][3].arrive()
+            second[i][2] = ring_start(b, 2, lo, hi)
+
+    z_parts = [i for i, part in enumerate(routes) if part[0] == "z"]
+    y_parts = [i for i, part in enumerate(routes) if part[0] == "y"]
 
     def accumulate(*blocks):
         for dy, dz in blocks:
@@ -370,7 +376,7 @@
     gmid[z_of] = gsend_t[y]
     mark("bwd_y")
 
-    gather_second(0)
+    gather_second(0, z_parts)
     for c in genz_in:
         c.arrive()
     fill_pairs(mats_z, gz)
@@ -380,11 +386,13 @@
     for d in range(1, 4):
         step_in.append(send(gmid.at[wrap(z + d, SIDE)], gzb.at[z], at(0, d)))
     gzb[z] = gmid[z]
+    mark("ag0")
+
+    gather_first(z_parts)
+    gather_first(y_parts)
+    gather_second(0, y_parts)
     w_copy.wait()
     base[...] = dot(hid[...], w_rows(0, 0))
-    mark("ag0")
-
-    gather_first()
     mark("ag1")
     for c in step_in:
         c.arrive()
@@ -395,11 +403,11 @@
     ghome[z] = gsend_z[z]
     mark("bwd_z")
 
-    gather_far()
+    gather_far(z_parts)
+    gather_second(1, z_parts)
+    gather_second(3, z_parts)
+    gather_far(y_parts)
     accumulate((1, 0), (3, 0), (0, 1), (0, 3))
-    gather_second(1)
-    gather_second(3)
-    accumulate((2, 0), (0, 2), (1, 1), (3, 1))
     mark("ag2")
 
     for c in back_in:
@@ -417,7 +425,10 @@
     gb[:, 256:] = fb.astype(BF16)
     mark("bwd_local")
 
-    gather_second(2)
+    gather_second(1, y_parts)
+    gather_second(3, y_parts)
+    gather_second(2, z_parts)
+    gather_second(2, y_parts)
     mark("ag3")
 
     computed = set()
@@ -506,7 +517,7 @@
 
     far(sums, 2, 1, 3, 0)
     mark("rs_far")
-    accumulate((1, 3), (3, 3), (1, 2), (3, 2))
+    accumulate((2, 0), (0, 2), (1, 1), (3, 1), (1, 3), (3, 3), (1, 2), (3, 2))
 
     accumulate((2, 1), (2, 3), (2, 2))
     mark("base")
@@ -556,9 +567,10 @@
         lambda d: wrap(z + d, SIDE),
     )
     mark("fwd_z")
-    near(sums, 3, 0)
+    near(sums, 3)
     for s in sums:
-        s.last_far()
+        if s.a == "y":
+            s.last_far()
     mark("near2")
 
     def pair_grads(states, grads, dst):
@@ -623,6 +635,10 @@
             for c in self.outs:
                 c.arrive()
 
+    near(sums, 0)
+    for s in sums:
+        if s.a == "z":
+            s.last_far()
     early, late = Slabs(0, 96, sums_a, slab_a), Slabs(1536, 32, sums_b, slab_b)
     for c in outz_in:
         c.arrive()

time: 157 us -> 159 us (1.013)
  Pallas kernels: 156 us -> 159 us
    pallas_call x1, Pallas kernels: 153 us -> 156 us  [main_call(): pl.pallas_call(functools.partial(main_kernel, n_dp, scale), out_shape=(ja...]
where the time goes in v8:
time: 159 us
  Pallas kernels  159 us (100%)
    pallas_call x1, Pallas kernels, main_call(): pl.pallas_call(functools.partial(main_kernel, n_dp, scale), out_shape=(ja...  156 us

profile of v8, /device:TPU:1, one launch (start us, length us, event | category | flops | bytes accessed | tf_op | source)
XLA Modules:
  0.0 159.3 jit_solution(8155917844404787878)
XLA Ops:
  0.6 155.9 %adapt.1 = (bf16[384,512]{1,0:T(8,128)(2,1)}, bf16[384,512]{1,0:T(8,128)(2,1)}, f32[8,64,512]{2,1,0:T(8,128)}) custom-call(bf16[384,512]{1,0:T(8,128)(2,1)} %refs_0_.1, bf16[8192,512]{1,0:T(8,128)(2,1)} %refs_1_.1, f32[8,64,512]{2,1,0:T(8,128)} %refs_2_.1, bf16[384,512]{1,0:T(8,128)(2,1)} %refs_3_.1), custom_call_target="tpu_custom_call" | custom-call | flops 6442450944 | bytes 12582912 | tf_op jit(solution)/shard_map/adapt/pallas_call | solution.py:684
  156.5 2.7 %results.1 = (bf16[384,512]{1,0:T(8,128)(2,1)}, bf16[384,512]{1,0:T(8,128)(2,1)}, f32[8,64,512]{2,1,0:T(8,128)}) custom-call(bf16[384,512]{1,0:T(8,128)(2,1)} %get-tuple-element.6.refs_0_, bf16[384,512]{1,0:T(8,128)(2,1)} %get-tuple-element.7.refs_1_, f32[8,64,512]{2,1,0:T(8,128)} %get-tuple-element.8.refs_2_), custom_call_target="tpu_custom_call" | custom-call | tf_op jit(solution)/shard_map/results/pallas_call | solution.py:748
